TPU v7x, 512 devices: a whole 4x4x16 slice. The times are simulated.
512 devices in a mesh: section: 4 (over x), expert: 128 (over z, y, core).
Axes of the slice: x: 4, y: 4, z: 16, core: 2. Of those that a mesh axis runs over, the one named last changes fastest.
Arguments:
- hidden_rows: bfloat16 [4, 1024, 3584], P('section', 'expert'), may hold values from -6 to 6
- expert_ids: int32 [4, 1024, 2], P('section', 'expert'), may hold values from 0 to 7, all different within a row; in each aligned block of 8 rows (0 to 7, 8 to 15, ..., all dimensions but the last counted through in order) at most 2 rows name the same one
- gate_weights: float32 [4, 1024, 2], P('section', 'expert'), may hold values from 0.2 to 2
- w_gate: bfloat16 [4, 3584, 16384], P('section', None, 'expert'), may hold values from -0.09375 to 0.09375
- w_up: bfloat16 [4, 3584, 16384], P('section', None, 'expert'), may hold values from -0.09375 to 0.09375
- w_down: bfloat16 [4, 16384, 3584], P('section', 'expert'), may hold values from -0.125 to 0.125
- query_latent: bfloat16 [4, 1024, 32, 512], P('section', 'expert')
- query_rope: bfloat16 [4, 1024, 2048], P('section', 'expert')
- cache_latent: bfloat16 [4, 8192, 512], P('section', 'expert'), may hold values from -4 to 4
- cache_rope: bfloat16 [4, 8192, 64], P('section', 'expert'), may hold values from -4 to 4
- offsets: int32 [4], P('section'), may hold values from 0 to 7168
Outputs:
- passed: bfloat16 [4, 1024, 3584], P('section', 'expert')
- attended: bfloat16 [4, 1024, 32, 512], P('section', 'expert')
Inputs may be any that keep to these rules, and one draw needn't show every extreme that they name: `expert_ids`: each row names 2 different experts. In every aligned block of 8 rows (the tokens of one device), no expert is named by more than 2 rows, a bound that some block reaches.
All inputs are finite; a program needn't handle non-finite values.
Results may differ from a plain program's by a relative error of at most 0.014.
Values may be sent and summed in bfloat16 or wider, within the bound.
A program may use at most 64 MiB of HBM per device.

v0:
```python
import jax
import jax.numpy as jnp
from jax import lax
from jax.sharding import PartitionSpec as P

EXPERTS = 8
TOP = 2


softmax_scale = 192.0 ** (-0.5)
masked_score = -1e30


def shifted(block, axis, distance):
    devices = range(lax.axis_size(axis))
    route = [((i - distance) % len(devices), i) for i in devices]
    return lax.ppermute(block, axis, route)


def attention(query_lat, query_rot, cache_lat, cache_rot, first_pos):
    local_count, head_count, latent_width = query_lat.shape
    rot_heads = query_rot.reshape(local_count, head_count, -1)
    positions = first_pos + jnp.arange(local_count, dtype=jnp.int32)
    running = jnp.full((local_count, head_count), masked_score, jnp.float32)
    lat_piece = lax.all_gather(cache_lat, "expert", axis=1, tiled=True)[0]
    rot_piece = lax.all_gather(cache_rot, "expert", axis=1, tiled=True)[0]
    scores = jnp.einsum("thl,jl->thj", query_lat, lat_piece, preferred_element_type=jnp.float32)
    scores = scores + jnp.einsum(
        "thr,jr->thj", rot_heads, rot_piece, preferred_element_type=jnp.float32
    )
    scores = scores * softmax_scale
    key_pos = jnp.arange(lat_piece.shape[0], dtype=jnp.int32)
    visible = key_pos[None, None, :] <= positions[:, None, None]
    highest = jnp.maximum(running, jnp.max(jnp.where(visible, scores, masked_score), axis=2))
    weights = jnp.where(
        visible, jnp.exp(jnp.where(visible, scores - highest[:, :, None], masked_score)), 0.0
    )
    totals = jnp.sum(weights, axis=2)
    partial_value = jnp.einsum(
        "thj,jl->thl", weights.astype(jnp.bfloat16), lat_piece, preferred_element_type=jnp.float32
    )
    running, totals, partial_value = (highest, totals, partial_value)
    return (partial_value / totals[:, :, None]).astype(jnp.bfloat16)


def expert_work(received, gate_cols, up_cols, down_rows):
    model_width = received.shape[2]
    flat_rows = received.reshape(-1, model_width)
    gate_val = jnp.dot(flat_rows, gate_cols, preferred_element_type=jnp.float32)
    up_val = jnp.dot(flat_rows, up_cols, preferred_element_type=jnp.float32)
    activated = (jax.nn.silu(gate_val) * up_val).astype(jnp.bfloat16)
    product = jnp.dot(activated, down_rows, preferred_element_type=jnp.float32).astype(jnp.bfloat16)
    return product.reshape(received.shape)


def per_device(
    hidden_rows,
    expert_ids,
    gate_weights,
    w_gate,
    w_up,
    w_down,
    query_latent,
    query_rope,
    cache_latent,
    cache_rope,
    offsets,
):
    local_rows = hidden_rows[0]
    token_count, model_width = local_rows.shape
    devices = lax.axis_size("expert")
    slices = devices // EXPERTS
    capacity = 5 * token_count * TOP // (4 * EXPERTS)
    first_pos = offsets[0] + lax.axis_index("expert") * token_count
    routing = expert_ids[0]
    gate_share = gate_weights[0]
    expert_range = jnp.arange(EXPERTS, dtype=jnp.int32)
    matches = routing[:, :, None] == expert_range[None, None, :]
    chosen = jnp.any(matches, axis=1).astype(jnp.int32)
    gate_of = jnp.sum(jnp.where(matches, gate_share[:, :, None], 0.0), axis=1)
    rank_in_expert = jnp.cumsum(chosen, axis=0) - chosen
    slot_range = jnp.arange(capacity, dtype=jnp.int32)
    slot_map = (chosen[:, :, None] == 1) & (rank_in_expert[:, :, None] == slot_range[None, None, :])
    packed = jnp.einsum(
        "tec,td->ecd", slot_map.astype(jnp.bfloat16), local_rows, preferred_element_type=jnp.float32
    ).astype(jnp.bfloat16)
    outgoing = jnp.broadcast_to(packed[:, None], (EXPERTS, slices, capacity, model_width)).reshape(
        devices, capacity, model_width
    )
    attended = attention(query_latent[0], query_rope[0], cache_latent, cache_rope, first_pos)
    returned = lax.all_to_all(
        expert_work(
            lax.all_to_all(outgoing, "expert", split_axis=0, concat_axis=0, tiled=True),
            w_gate[0],
            w_up[0],
            w_down[0],
        ),
        "expert",
        split_axis=0,
        concat_axis=0,
        tiled=True,
    )
    summed = jnp.sum(
        returned.reshape(EXPERTS, slices, capacity, model_width).astype(jnp.float32), axis=1
    )
    scaled = slot_map.astype(jnp.float32) * gate_of[:, :, None]
    mixture = jnp.einsum("tec,ecd->td", scaled, summed, precision=lax.Precision.HIGHEST)
    result = (local_rows.astype(jnp.float32) + mixture).astype(jnp.bfloat16)
    passed = shifted(result, "section", 1)
    return (passed[None], attended[None])


def solution(mesh):
    placed = (
        P("section", "expert", None),
        P("section", "expert", None),
        P("section", "expert", None),
        P("section", None, "expert"),
        P("section", None, "expert"),
        P("section", "expert", None),
        P("section", "expert", None, None),
        P("section", "expert", None),
        P("section", "expert", None),
        P("section", "expert", None),
        P("section"),
    )
    return jax.shard_map(
        per_device,
        mesh=mesh,
        in_specs=placed,
        out_specs=(P("section", "expert", None), P("section", "expert", None, None)),
        check_vma=False,
    )
```

profile of v0, /device:TPU:24, one launch (start us, length us, event | category | flops | bytes accessed | tf_op | source)
XLA Modules:
  0.0 355.5 jit_solution(16052382496482879596)
XLA Ops:
  7.2 0.0 copy-start
  7.2 0.0 all-gather.5.cloned.1.call-start
  7.2 1.4 copy.28
  8.7 0.0 all-gather.5.cloned.1.call-update
  8.7 0.8 fusion.46
  9.5 1.0 convolution_convert_fusion.1
  10.5 0.1 copy.26
  10.6 2.2 broadcast_in_dim.63
  12.8 19.7 %all-to-all-start = ((bf16[128,2,3584]{2,1,0:T(2,128)(2,1)}), bf16[128,2,3584]{2,1,0:T(2,128)(2,1)}, u32[]{:S(2)}, u32[]{:S(2)}) async-start(bf16[128,2,3584]{2,1,0:T(2,128)(2,1)} %bitcast.4), calls=%async_computation | async-start | bytes 3670016 | tf_op jit(solution)/shard_map/all_to_all | solution.py:93
  32.5 0.0 all-gather.3.cloned.1.call-start
  32.6 0.7 all-gather.3.cloned.1.call-update
  33.3 87.9 %all-to-all-done = bf16[128,2,3584]{2,1,0:T(2,128)(2,1)} async-done(((bf16[128,2,3584]{2,1,0:T(2,128)(2,1)}), bf16[128,2,3584]{2,1,0:T(2,128)(2,1)}, u32[]{:S(2)}, u32[]{:S(2)}) %all-to-all-start) | async-done | bytes 1835040 | tf_op jit(solution)/shard_map/all_to_all | solution.py:93
  121.1 4.1 %reshape.67 = bf16[256,3584]{1,0:T(8,128)(2,1)S(1)} reshape(bf16[128,2,3584]{2,1,0:T(2,128)(2,1)} %all-to-all-done) | data formatting | bytes 3670016 | tf_op jit(solution)/shard_map/reshape | solution.py:48
  125.2 0.0 copy-start.4
  125.2 0.0 copy-start.5
  125.2 0.0 copy-start.2
  125.2 1.8 fusion.34
  127.1 0.0 copy-done
  127.1 0.0 copy-start.3
  127.1 3.6 %convolution_convert_fusion = bf16[256,3584]{1,0:T(8,128)(2,1)} fusion(bf16[256,3584]{1,0:T(8,128)(2,1)S(1)} %reshape.67, bf16[1,128,3584]{2,1,0:T(8,128)(2,1)S(1)} %copy-done, bf16[1,3584,128]{2,1,0:T(8,128)(2,1)} %param.15, f32[256,128]{1,0:T(8,128)S(1)} %fusion.34), kind=kOutput, calls=%fused_computation.10 | convolution fusion | flops 470876160 | bytes 5636096 | tf_op jit(solution)/shard_map/dot_general | solution.py:52
  130.7 0.0 copy-start.1
  130.7 4.8 %reshape.68 = bf16[128,2,3584]{2,1,0:T(2,128)(2,1)} reshape(bf16[256,3584]{1,0:T(8,128)(2,1)} %convolution_convert_fusion) | data formatting | bytes 3670016 | tf_op jit(solution)/shard_map/reshape | solution.py:53
  135.5 9.7 %all-to-all-start.1 = ((bf16[128,2,3584]{2,1,0:T(2,128)(2,1)}), bf16[128,2,3584]{2,1,0:T(2,128)(2,1)S(1)}, u32[]{:S(2)}, u32[]{:S(2)}) async-start(bf16[128,2,3584]{2,1,0:T(2,128)(2,1)} %reshape.68), calls=%async_computation.1 | async-start | bytes 3670016 | tf_op jit(solution)/shard_map/all_to_all | solution.py:91
  145.9 0.0 copy-done.4
  145.9 0.0 copy-done.5
  145.9 0.1 select_reduce_fusion.1
  146.0 90.3 %all-to-all-done.1 = bf16[128,2,3584]{2,1,0:T(2,128)(2,1)S(1)} async-done(((bf16[128,2,3584]{2,1,0:T(2,128)(2,1)}), bf16[128,2,3584]{2,1,0:T(2,128)(2,1)S(1)}, u32[]{:S(2)}, u32[]{:S(2)}) %all-to-all-start.1) | async-done | bytes 1835040 | tf_op jit(solution)/shard_map/all_to_all | solution.py:91
  236.3 1.5 convert_reduce_fusion
  237.7 0.0 copy-done.2
  237.8 0.3 fusion.8
  238.1 4.3 %collective-permute-start = (bf16[8,3584]{1,0:T(8,128)(2,1)S(1)}, bf16[8,3584]{1,0:T(8,128)(2,1)S(1)}, u32[]{:S(2)}, u32[]{:S(2)}) collective-permute-start(bf16[8,3584]{1,0:T(8,128)(2,1)S(1)} %fusion.8), channel_id=1, source_target_pairs={{384,0},{0,128},{128,256},{256,384},{385,1},{1,129},{129,257},{257... | collective-permute-start | bytes 172040 | tf_op jit(solution)/shard_map/ppermute | solution.py:17
  242.4 0.1 iota_compare_fusion
  242.5 0.0 copy-done.3
  242.5 0.1 reshape_squeeze.3
  242.6 0.0 all-gather.5.cloned.1.call-done
  242.7 9.0 %copy.29 = bf16[1,8192,64]{1,2,0:T(8,128)(2,1)} copy(bf16[1,8192,64]{2,0,1:T(2,128)(2,1)} %all-gather.5.cloned.1.call-done) | data formatting | bytes 2097152 | tf_op jit(solution)/shard_map/all_gather | solution.py:26
  251.6 0.0 collective-permute-done
  251.6 80.8 %all-gather.3.cloned.1.call-done = bf16[1,8192,512]{2,1,0:T(8,128)(2,1)} async-done(((bf16[1,64,512]{2,1,0:T(8,128)(2,1)}), bf16[1,8192,512]{2,1,0:T(8,128)(2,1)}) %all-gather.3.cloned.1.call-update) | async-done | bytes 8388624 | tf_op jit(solution)/shard_map/all_gather | solution.py:25
  332.5 0.0 copy-done.1
  332.5 0.0 slice-start
  332.5 6.0 %fusion.3 = f32[8,32,8192]{2,1,0:T(8,128)S(1)} fusion(bf16[1,8192,512]{2,1,0:T(8,128)(2,1)} %all-gather.3.cloned.1.call-done, bf16[1,8,32,512]{3,2,1,0:T(8,128)(2,1)S(1)} %copy-done.1), kind=kOutput, calls=%fused_computation.4 | convolution fusion | flops 2147483648 | bytes 17039360 | tf_op jit(solution)/shard_map/thl,jl->thj/dot_general | solution.py:27
  338.5 0.0 slice-start.1
  338.5 3.8 %select_reduce_fusion = (f32[8,32]{1,0:T(8,128)S(1)}, f32[8,32,8192]{2,1,0:T(8,128)S(1)}) fusion(pred[8,8192]{1,0:T(8,128)(4,1)S(1)} %iota_compare_fusion, f32[8,32,8192]{2,1,0:T(8,128)S(1)} %fusion.3, bf16[8,32,64]{2,1,0:T(8,128)(2,1)S(1)} %reshape_squeeze.3, bf16[1,8192,64]{1,2,0:T(8,128)(2,1)} %copy.29), kind=kOutput, calls=%fused_computation.7 | convolution fusion | flops 276823808 | bytes 17925120 | tf_op jit(solution)/shard_map/thr,jr->thj/dot_general | solution.py:28
  342.3 2.6 fusion.5
  344.9 0.0 slice-done
  344.9 0.0 slice-done.1
  344.9 3.1 fusion.26
  348.1 0.6 copy.35
  (6 shorter events, 0.0 us)
Async XLA Ops:
  7.2 119.9 %copy-start = (bf16[1,128,3584]{2,1,0:T(8,128)(2,1)S(1)}, bf16[1,128,3584]{2,1,0:T(8,128)(2,1)}, u32[]{:S(2)}) copy-start(bf16[1,128,3584]{2,1,0:T(8,128)(2,1)} %param.16) | copy-start | bytes 2752516
  7.2 235.5 %all-gather.5.cloned.1.call-start = ((), (), s32[]{:S(2)}) async-start(), calls=%async_computation.3 | async-start | bytes 4227072 | tf_op jit(solution)/shard_map/all_gather | solution.py:26
  12.8 108.3 %all-to-all-start = ((bf16[128,2,3584]{2,1,0:T(2,128)(2,1)}), bf16[128,2,3584]{2,1,0:T(2,128)(2,1)}, u32[]{:S(2)}, u32[]{:S(2)}) async-start(bf16[128,2,3584]{2,1,0:T(2,128)(2,1)} %bitcast.4), calls=%async_computation | async-start | bytes 3670016 | tf_op jit(solution)/shard_map/all_to_all | solution.py:93
  32.5 300.0 %all-gather.3.cloned.1.call-start = ((), (), s32[]{:S(2)}) async-start(), calls=%async_computation.2 | async-start | bytes 8454144 | tf_op jit(solution)/shard_map/all_gather | solution.py:25
  125.2 20.7 %copy-start.4 = (s32[1,8,2]{1,2,0:T(2,128)S(1)}, s32[1,8,2]{1,2,0:T(2,128)}, u32[]{:S(2)}) copy-start(s32[1,8,2]{1,2,0:T(2,128)} %param.12) | copy-start | bytes 196
  125.2 20.7 %copy-start.5 = (f32[1,8,2]{1,2,0:T(2,128)S(1)}, f32[1,8,2]{1,2,0:T(2,128)}, u32[]{:S(2)}) copy-start(f32[1,8,2]{1,2,0:T(2,128)} %param.13) | copy-start | bytes 196
  125.2 112.5 %copy-start.2 = (bf16[1,8,3584]{2,1,0:T(8,128)(2,1)S(1)}, bf16[1,8,3584]{2,1,0:T(8,128)(2,1)}, u32[]{:S(2)}) copy-start(bf16[1,8,3584]{2,1,0:T(8,128)(2,1)} %param.11) | copy-start | bytes 172036
  127.1 115.4 %copy-start.3 = (bf16[1,8,2048]{2,1,0:T(8,128)(2,1)S(1)}, bf16[1,8,2048]{2,1,0:T(8,128)(2,1)}, u32[]{:S(2)}) copy-start(bf16[1,8,2048]{2,1,0:T(8,128)(2,1)} %param.18) | copy-start | bytes 98308
  130.7 201.8 %copy-start.1 = (bf16[1,8,32,512]{3,2,1,0:T(8,128)(2,1)S(1)}, bf16[1,8,32,512]{3,2,1,0:T(8,128)(2,1)}, u32[]{:S(2)}) copy-start(bf16[1,8,32,512]{3,2,1,0:T(8,128)(2,1)} %param.17) | copy-start | bytes 786436
  135.5 100.7 %all-to-all-start.1 = ((bf16[128,2,3584]{2,1,0:T(2,128)(2,1)}), bf16[128,2,3584]{2,1,0:T(2,128)(2,1)S(1)}, u32[]{:S(2)}, u32[]{:S(2)}) async-start(bf16[128,2,3584]{2,1,0:T(2,128)(2,1)} %reshape.68), calls=%async_computation.1 | async-start | bytes 3670016 | tf_op jit(solution)/shard_map/all_to_all | solution.py:91
  238.1 13.6 %collective-permute-start = (bf16[8,3584]{1,0:T(8,128)(2,1)S(1)}, bf16[8,3584]{1,0:T(8,128)(2,1)S(1)}, u32[]{:S(2)}, u32[]{:S(2)}) collective-permute-start(bf16[8,3584]{1,0:T(8,128)(2,1)S(1)} %fusion.8), channel_id=1, source_target_pairs={{384,0},{0,128},{128,256},{256,384},{385,1},{1,129},{129,257},{257... | collective-permute-start | bytes 172040 | tf_op jit(solution)/shard_map/ppermute | solution.py:17
  332.5 12.4 %slice-start = ((s8[8388608]{0:T(1024)(128)(4,1)}), s8[4194304]{0:T(1024)(128)(4,1)S(1)}, s32[]{:S(2)}) async-start(s8[8388608]{0:T(1024)(128)(4,1)} %bitcast.56), calls=%async_computation.4 | async-start | bytes 8388608
  338.5 6.4 %slice-start.1 = ((s8[8388608]{0:T(1024)(128)(4,1)}), s8[4194304]{0:T(1024)(128)(4,1)S(1)}, s32[]{:S(2)}) async-start(s8[8388608]{0:T(1024)(128)(4,1)} %bitcast.56), calls=%async_computation.5 | async-start | bytes 8388608
Sparse Core Ops, SparseCore 0:
  11.7 164.4 all-gather.4
  179.3 153.1 all-gather.2
where the time goes:
time: 360 us; the launch traced here: 356 us
  waiting for transfers between devices  260 us (72%)
  starting transfers between devices  33.7 us (9%)
  local copies, waits for them, and re-layouts  22.4 us (6%)
  matrix products  19.7 us (5%)
  between operations  14.9 us (4%)
  other arithmetic  5.07 us (1%)
    all_to_all x1, waiting for transfers between devices, per_device(): lax.all_to_all(expert_work(lax.all_to_all(outgoing, 'expert', split_axis=...  90.3 us
    all_to_all x1, waiting for transfers between devices, per_device(): lax.all_to_all(outgoing, 'expert', split_axis=0, concat_axis=0, tiled=True)  87.9 us
    all_gather x1, waiting for transfers between devices, attention(): lat_piece = lax.all_gather(cache_lat, 'expert', axis=1, tiled=True)[0]  80.8 us
    all_to_all x1, starting transfers between devices, per_device(): lax.all_to_all(outgoing, 'expert', split_axis=0, concat_axis=0, tiled=True)  19.7 us
    all_to_all x1, starting transfers between devices, per_device(): lax.all_to_all(expert_work(lax.all_to_all(outgoing, 'expert', split_axis=...  9.67 us
    all_gather x1, local copies, waits for them, and re-layouts, attention(): rot_piece = lax.all_gather(cache_rot, 'expert', axis=1, tiled=True)[0]  8.98 us
  transfers between devices with their start and end apart: 5, of which 3 were waited for; matrix products, arithmetic and copies ran while one was open for 8% of the time, Pallas kernels for 0%

commit v1 on v0

v1 whole, which is shorter than its diff:
```python
import functools
import math

import jax
import jax.numpy as jnp
from jax import lax
from jax.experimental import pallas as pl
from jax.experimental.pallas import tpu as pltpu
from jax.sharding import PartitionSpec as P

MESH = pl.DeviceIdType.MESH
EXPERTS = 8
NZ, NY = 16, 4
TOKENS, HEADS = 8, 32
ROWS = TOKENS * HEADS
LATENT, ROPE = 512, 64
KEYS = 64
KW = LATENT + 128
WIDTH = 3584
COLS = WIDTH // NY
HALF = NZ // 2
NEAR = NZ // 4
scale_log2 = 192.0 ** (-0.5) * math.log2(math.e)
masked_score = -1e30
f32, bf16 = jnp.float32, jnp.bfloat16


def slot_of(r):
    return (r + NEAR) % NZ


def kernel(
    x_ref, ids_ref, gate_ref, wg_ref, wu_ref, wd_ref, q_ref, qrope_ref, klat_ref, krope_ref, offset_ref,
    passed_ref, out_ref,
    kbuf, ql, qraw, qr, rel, acc, m_ref, l_ref, o_send, o_recv, ls_send, ls_recv,
    xs, xs_recv, g_recv, packed, xall, wgu, wd, csib_send, csib_recv, own_sum, cy_send, cy_recv, csum, ret, fin, fin_recv,
    send_ring, recv_ring, send_sib, recv_sib, send_q, recv_q, send_o, recv_o,
    send_d1, recv_d1, send_d2, recv_d2, send_d3, recv_d3, send_d3s, recv_d3s,
    send_c0, recv_c0, send_c1, recv_c1, send_c2, recv_c2, send_fin, recv_fin, sem_w, sem_l,
):
    sec = lax.axis_index("section")
    nsec = lax.axis_size("section")
    me = lax.axis_index("expert")
    c = lax.rem(me, 2)
    y = lax.rem(lax.div(me, 2), NY)
    z = lax.div(me, 2 * NY)
    sib = me + 1 - 2 * c

    def at(zz, yy):
        return (sec, (zz * NY + yy) * 2 + c)

    def zplus(r):
        return lax.rem(z + (r % NZ), NZ)

    def yplus(d):
        return lax.rem(y + (d % NY), NY)

    next_sec = lax.rem(sec + 1, nsec)
    prev_sec = lax.rem(sec + nsec - 1, nsec)
    sends = []

    def send(src, dst, ssem, rsem, device):
        copy = pltpu.make_async_remote_copy(
            src_ref=src, dst_ref=dst, send_sem=ssem, recv_sem=rsem, device_id=device, device_id_type=MESH
        )
        copy.start()
        sends.append(copy)

    def arrived(ref, sem):
        pltpu.make_async_copy(ref, ref, sem).wait()

    barrier = pltpu.get_barrier_semaphore()

    def greet(device):
        pl.semaphore_signal(barrier, inc=1, device_id=device, device_id_type=MESH)

    greet((sec, sib))
    for d in range(1, NY):
        greet(at(z, yplus(d)))
    for r in range(1, NZ):
        greet(at(zplus(r), y))
    for d in range(NY):
        greet((prev_sec, (z * NY + d) * 2 + c))

    locals_ = [pltpu.make_async_copy(q_ref, ql.at[0], sem_l.at[0])]
    for k in range(NY):
        rows = pl.ds(k * COLS, COLS)
        locals_.append(pltpu.make_async_copy(wg_ref.at[rows, :], wgu.at[k, :, pl.ds(0, 128)], sem_w.at[k, 0]))
        locals_.append(pltpu.make_async_copy(wu_ref.at[rows, :], wgu.at[k, :, pl.ds(128, 128)], sem_w.at[k, 1]))
        locals_.append(pltpu.make_async_copy(wd_ref.at[:, rows], wd.at[k], sem_w.at[k, 2]))
    for copy in locals_:
        copy.start()

    for k in range(NY):
        xs[k] = x_ref[:, k * COLS : (k + 1) * COLS]
    kbuf[0, 0, :, :LATENT] = klat_ref[...]
    kbuf[0, 0, :, LATENT:] = jnp.concatenate([krope_ref[...], jnp.zeros((KEYS, 128 - ROPE), bf16)], axis=1)

    lane = lax.broadcasted_iota(jnp.int32, (TOKENS, 128), 1)
    token = lax.broadcasted_iota(jnp.int32, (TOKENS, 128), 0)
    lane_e, lane_y, lane_rank = lane >> 3, (lane >> 1) & 3, lane & 1
    first, second = ids_ref[:, 0:1] == lane_e, ids_ref[:, 1:2] == lane_e
    hit = jnp.where(first | second, 1, 0)
    rank = jnp.zeros((TOKENS, 128), jnp.int32)
    for t in range(TOKENS - 1):
        rank = rank + jnp.where(token > t, hit[t : t + 1, :], 0)
    share = jnp.where(first, gate_ref[:, 0:1], gate_ref[:, 1:2])
    g_recv[0] = jnp.where((hit == 1) & (rank == lane_rank) & (lane_y == y), share, 0.0)
    xs_recv[0] = xs[y]

    pl.semaphore_wait(barrier, 1 + (NY - 1) + (NZ - 1) + NY)

    for d in range(1, NY):
        to = at(z, yplus(d))
        send(xs.at[yplus(d)], xs_recv.at[NY - d], send_d1.at[0, d], recv_d1.at[0], to)
        send(g_recv.at[0], g_recv.at[NY - d], send_d1.at[1, d], recv_d1.at[1], to)
    send(kbuf.at[0, 0], kbuf.at[1, 0], send_ring.at[0, 0], recv_ring.at[0, 1], at(zplus(1), y))
    send(kbuf.at[0, 0], kbuf.at[1, 2], send_ring.at[1, 0], recv_ring.at[1, 1], at(zplus(-1), y))
    send(kbuf.at[0, 0], kbuf.at[0, 1], send_sib.at[0, 0], recv_sib.at[0, 0], (sec, sib))
    for d in (1, 3, 2):
        to = at(z, yplus(d))
        send(q_ref, ql.at[NY - d], send_q.at[0, d], recv_q.at[0, NY - d], to)
        send(qrope_ref, qraw.at[NY - d], send_q.at[1, d], recv_q.at[1, NY - d], to)

    arrived(xs_recv.at[pl.ds(1, NY - 1)], recv_d1.at[0])
    arrived(g_recv.at[pl.ds(1, NY - 1)], recv_d1.at[1])
    gates = g_recv[...].reshape(NY * TOKENS, 128)
    pick = jnp.where(jnp.transpose(gates)[: 8 * EXPERTS] != 0.0, 1.0, 0.0).astype(bf16)
    plane = xs_recv[...].astype(f32).reshape(NY * TOKENS, COLS).astype(bf16)
    packed[...] = jnp.dot(pick, plane, preferred_element_type=f32).reshape(EXPERTS, 8, COLS).astype(bf16)
    mine = pltpu.make_async_copy(packed.at[lax.div(z, 2)], xall.at[0, 0, slot_of(0)], recv_d2.at[0])
    mine.start()
    for r in sorted(range(1, NZ), key=lambda r: min(r, NZ - r)):
        slot = slot_of(-r)
        send(
            packed.at[lax.div(zplus(r), 2)], xall.at[0, 0, slot], send_d2.at[r], recv_d2.at[slot // HALF], at(zplus(r), y)
        )

    def ring(s):
        if s < HALF:
            arrived(kbuf.at[s, 0], recv_ring.at[0, s])
            arrived(kbuf.at[s, 2], recv_ring.at[1, s])
            if s < HALF - 1:
                send(kbuf.at[s, 0], kbuf.at[s + 1, 0], send_ring.at[0, s], recv_ring.at[0, s + 1], at(zplus(1), y))
                send(kbuf.at[s, 2], kbuf.at[s + 1, 2], send_ring.at[1, s], recv_ring.at[1, s + 1], at(zplus(-1), y))
            else:
                low, high = pl.ds(0, KEYS // 2), pl.ds(KEYS // 2, KEYS // 2)
                send(
                    kbuf.at[s, 0, low], kbuf.at[0, 2, low], send_ring.at[0, s], recv_ring.at[0, s + 1], at(zplus(1), y)
                )
                send(
                    kbuf.at[s, 2, high], kbuf.at[0, 2, high], send_ring.at[1, s], recv_ring.at[1, s + 1], at(zplus(-1), y)
                )
            send(kbuf.at[s, 0], kbuf.at[s, 1], send_sib.at[0, s], recv_sib.at[0, s], (sec, sib))
            send(kbuf.at[s, 2], kbuf.at[s, 3], send_sib.at[1, s], recv_sib.at[1, s], (sec, sib))
        else:
            arrived(kbuf.at[0, 2, pl.ds(0, KEYS // 2)], recv_ring.at[0, s])
            arrived(kbuf.at[0, 2, pl.ds(KEYS // 2, KEYS // 2)], recv_ring.at[1, s])
            send(kbuf.at[0, 2], kbuf.at[0, 3], send_sib.at[1, 0], recv_sib.at[1, 0], (sec, sib))

    def spread_rope():
        keep = lax.broadcasted_iota(jnp.int32, (TOKENS, 128), 1) < ROPE

        def one(d, carry):
            for h in range(HEADS):
                pair = qraw[d, :, (h // 2) * 128 : (h // 2 + 1) * 128].astype(f32)
                if h % 2:
                    pair = pltpu.roll(pair, ROPE, 1)
                rel[pl.ds(h, TOKENS, stride=HEADS), :] = jnp.where(keep, pair, 0.0)
            qr[d] = rel[...].astype(bf16)
            return carry

        lax.fori_loop(0, NY, one, 0)

    def attend(s, first):
        arrived(kbuf.at[s, 1], recv_sib.at[0, s])
        arrived(kbuf.at[s, 3], recv_sib.at[1, s])
        lanes = lax.broadcasted_iota(jnp.int32, (1, 1, 4 * KEYS), 2)
        block, inside = lanes // KEYS, lanes % KEYS
        za, zb = (z, zplus(HALF)) if s == 0 else (zplus(-s), zplus(s))
        zz = jnp.where(block < 2, za, zb)
        cc = jnp.where(block % 2 == 0, c, 1 - c)
        key_pos = ((zz * NY + y) * 2 + cc) * KEYS + inside
        kc = kbuf[s].reshape(4 * KEYS, KW)
        k_lat, k_rope = kc[:, :LATENT], kc[:, LATENT:]
        token_of = lax.broadcasted_iota(jnp.int32, (TOKENS, 1, 1), 0)

        def one(d, carry):
            owner = (z * NY + lax.rem(y + d, NY)) * 2 + c
            position = offset_ref[0] + owner * TOKENS + token_of
            cap = jnp.where(key_pos <= position, jnp.inf, masked_score)
            contract = (((1,), (1,)), ((), ()))
            score = lax.dot_general(ql[d], k_lat, contract, preferred_element_type=f32)
            score = score + lax.dot_general(qr[d], k_rope, contract, preferred_element_type=f32)
            score = jnp.minimum(score.reshape(TOKENS, HEADS, 4 * KEYS), cap).reshape(ROWS, 4 * KEYS)
            left, right = score[:, :128], score[:, 128:]
            top = jnp.max(jnp.maximum(left, right), axis=1, keepdims=True)
            if first:
                new = jnp.broadcast_to(top, (ROWS, 128))
            else:
                old = m_ref[d]
                new = jnp.maximum(old, top)
                alpha = jnp.exp2((old - new) * scale_log2)
            left = jnp.exp2((left - new) * scale_log2)
            right = jnp.exp2((right - new) * scale_log2)
            weights = jnp.concatenate([left.astype(bf16), right.astype(bf16)], axis=1)
            value = jnp.dot(weights, k_lat, preferred_element_type=f32)
            m_ref[d] = new
            if first:
                l_ref[d] = left + right
                acc[d] = value
            else:
                l_ref[d] = l_ref[d] * alpha + left + right
                acc[d] = acc[d] * jnp.concatenate([alpha] * (LATENT // 128), axis=1) + value
            return carry

        lax.fori_loop(0, NY, one, 0)

    def spread(half):
        part = pl.ds(half * HALF, HALF)
        arrived(xall.at[0, 0, part], recv_d2.at[half])
        for d in (1, 3, 2):
            send(
                xall.at[0, 0, part], xall.at[NY - d, 0, part], send_d3.at[half, d], recv_d3.at[half, NY - d],
                at(z, yplus(d)),
            )
        send(xall.at[0, 0, part], xall.at[0, 1, part], send_d3s.at[half, 0], recv_d3s.at[half, 0], (sec, sib))

    def share_rows(half):
        part = pl.ds(half * HALF, HALF)
        for d in (1, 3, 2):
            arrived(xall.at[d, 0, part], recv_d3.at[half, d])
            send(xall.at[d, 0, part], xall.at[d, 1, part], send_d3s.at[half, d], recv_d3s.at[half, d], (sec, sib))

    n_rows = HALF * 8

    def experts(half):
        part = pl.ds(half * HALF, HALF)
        total = None
        for d in range(NY):
            arrived(xall.at[d, 1, part], recv_d3s.at[half, d])
            rows = xall[d, :, half * HALF : (half + 1) * HALF].astype(f32).reshape(2 * n_rows, COLS).astype(bf16)
            term = jnp.dot(rows, wgu[yplus(d)], preferred_element_type=f32)
            total = term if total is None else total + term
        gate, up = total[:, :128], total[:, 128:]
        active = (gate / (1.0 + jnp.exp(-gate)) * up).astype(bf16)
        for d in range(NY):
            piece = jnp.dot(active, wd[yplus(d)], preferred_element_type=f32).reshape(2, HALF, 8, COLS)
            own_sum[half, d] = piece[0]
            csib_send[half, d] = piece[1].astype(bf16)
        send(csib_send.at[half], csib_recv.at[half], send_c0.at[half], recv_c0.at[half], (sec, sib))

    def combine(half):
        arrived(csib_recv.at[half], recv_c0.at[half])
        for d in (1, 3, 2):
            cy_send[half, d - 1] = (own_sum[half, d] + csib_recv[half, d].astype(f32)).astype(bf16)
            send(
                cy_send.at[half, d - 1], cy_recv.at[half, NY - d - 1], send_c1.at[half, d], recv_c1.at[half, NY - d],
                at(z, yplus(d)),
            )

    def give_back(half):
        total = own_sum[half, 0] + csib_recv[half, 0].astype(f32)
        for d in range(1, NY):
            arrived(cy_recv.at[half, d - 1], recv_c1.at[half, d])
            total = total + cy_recv[half, d - 1].astype(f32)
        csum[half] = total.astype(bf16)
        for slot in range(half * HALF, (half + 1) * HALF):
            r = (slot - NEAR) % NZ
            block = csum.at[half, slot - half * HALF]
            if r == 0:
                back = pltpu.make_async_copy(block, ret.at[z], recv_c2)
                back.start()
            else:
                send(block, ret.at[z], send_c2.at[r], recv_c2, at(zplus(r), y))

    def finish():
        arrived(ret, recv_c2)
        pairs = ret[...].astype(f32).reshape(EXPERTS, 2, 8, COLS)
        rows = (pairs[:, 0] + pairs[:, 1]).reshape(8 * EXPERTS, COLS)
        weights = g_recv[...].reshape(NY * TOKENS, 128)[:, : 8 * EXPERTS]
        mixture = jnp.dot(weights, rows, precision=lax.Precision.HIGHEST, preferred_element_type=f32)
        result = mixture.reshape(NY, TOKENS, COLS) + xs_recv[...].astype(f32)
        fin[...] = result.astype(bf16)
        for d in range(NY):
            to = (next_sec, (z * NY + yplus(d)) * 2 + c)
            send(fin.at[d], fin_recv.at[y], send_fin.at[d], recv_fin, to)

    def close(d):
        total = jnp.sum(l_ref[d], axis=1, keepdims=True)
        level = m_ref[d] * scale_log2 + jnp.log2(total)
        return level, acc[d] / total

    def give_out():
        for d in (2, 1, 3):
            level, value = close(d)
            o_send[d - 1] = value.astype(bf16)
            ls_send[d - 1] = jnp.transpose(level)[:8, :]
            to = at(z, yplus(d))
            send(o_send.at[d - 1], o_recv.at[NY - d - 1], send_o.at[0, d], recv_o.at[0, NY - d], to)
            send(ls_send.at[d - 1], ls_recv.at[NY - d - 1], send_o.at[1, d], recv_o.at[1, NY - d], to)

    def merge():
        level, value = close(0)
        levels, values = [level], [value]
        for d in range(1, NY):
            arrived(o_recv.at[d - 1], recv_o.at[0, d])
            arrived(ls_recv.at[d - 1], recv_o.at[1, d])
            levels.append(jnp.transpose(jnp.broadcast_to(ls_recv[d - 1][0:1, :], (128, ROWS))))
        best = functools.reduce(jnp.maximum, levels)
        shares = [jnp.exp2(one - best) for one in levels]
        norm = 1.0 / functools.reduce(jnp.add, shares)
        total = value * jnp.concatenate([shares[0] * norm] * (LATENT // 128), axis=1)
        for d in range(1, NY):
            factor = jnp.concatenate([shares[d] * norm] * (LATENT // 128), axis=1)
            total = total + o_recv[d - 1].astype(f32) * factor
        out_ref[...] = total.astype(bf16)

    ring(1)
    ring(2)
    spread(0)
    qraw[0] = qrope_ref[...]
    ring(3)
    for d in (1, 3, 2):
        arrived(ql.at[d], recv_q.at[0, d])
        arrived(qraw.at[d], recv_q.at[1, d])
    locals_[0].wait()
    spread_rope()
    ring(4)
    attend(1, True)
    spread(1)
    ring(5)
    share_rows(0)
    attend(2, False)
    ring(6)
    for copy in locals_[1:]:
        copy.wait()
    experts(0)
    ring(7)
    attend(3, False)
    combine(0)
    ring(8)
    share_rows(1)
    attend(4, False)
    experts(1)
    attend(5, False)
    combine(1)
    give_back(0)
    attend(6, False)
    attend(7, False)
    attend(0, False)
    give_back(1)
    give_out()
    finish()
    merge()
    arrived(fin_recv, recv_fin)
    for k in range(NY):
        passed_ref[:, k * COLS : (k + 1) * COLS] = fin_recv[k]
    for copy in sends:
        copy.wait_send()


def per_device(
    hidden_rows, expert_ids, gate_weights, w_gate, w_up, w_down, query_latent, query_rope, cache_latent, cache_rope, offsets
):
    vmem = pl.BlockSpec(memory_space=pltpu.VMEM)
    anywhere = pl.BlockSpec(memory_space=pl.ANY)
    dma = pltpu.SemaphoreType.DMA
    passed, attended = pl.pallas_call(
        kernel,
        out_shape=(
            jax.ShapeDtypeStruct((TOKENS, WIDTH), bf16),
            jax.ShapeDtypeStruct((ROWS, LATENT), bf16),
        ),
        in_specs=[
            vmem, vmem, vmem, anywhere, anywhere, anywhere, anywhere, vmem, vmem, vmem,
            pl.BlockSpec(memory_space=pltpu.SMEM),
        ],
        out_specs=(vmem, vmem),
        scratch_shapes=[
            pltpu.VMEM((HALF, 4, KEYS, KW), bf16),
            pltpu.VMEM((NY, ROWS, LATENT), bf16),
            pltpu.VMEM((NY, TOKENS, HEADS * ROPE), bf16),
            pltpu.VMEM((NY, ROWS, 128), bf16),
            pltpu.VMEM((ROWS, 128), f32),
            pltpu.VMEM((NY, ROWS, LATENT), f32),
            pltpu.VMEM((NY, ROWS, 128), f32),
            pltpu.VMEM((NY, ROWS, 128), f32),
            pltpu.VMEM((NY - 1, ROWS, LATENT), bf16),
            pltpu.VMEM((NY - 1, ROWS, LATENT), bf16),
            pltpu.VMEM((NY - 1, 8, ROWS), f32),
            pltpu.VMEM((NY - 1, 8, ROWS), f32),
            pltpu.VMEM((NY, TOKENS, COLS), bf16),
            pltpu.VMEM((NY, TOKENS, COLS), bf16),
            pltpu.VMEM((NY, TOKENS, 128), f32),
            pltpu.VMEM((EXPERTS, 8, COLS), bf16),
            pltpu.VMEM((NY, 2, NZ, 8, COLS), bf16),
            pltpu.VMEM((NY, COLS, 256), bf16),
            pltpu.VMEM((NY, 128, COLS), bf16),
            pltpu.VMEM((2, NY, HALF, 8, COLS), bf16),
            pltpu.VMEM((2, NY, HALF, 8, COLS), bf16),
            pltpu.VMEM((2, NY, HALF, 8, COLS), f32),
            pltpu.VMEM((2, NY - 1, HALF, 8, COLS), bf16),
            pltpu.VMEM((2, NY - 1, HALF, 8, COLS), bf16),
            pltpu.VMEM((2, HALF, 8, COLS), bf16),
            pltpu.VMEM((NZ, 8, COLS), bf16),
            pltpu.VMEM((NY, TOKENS, COLS), bf16),
            pltpu.VMEM((NY, TOKENS, COLS), bf16),
            dma((2, HALF)), dma((2, HALF + 1)),
            dma((2, HALF)), dma((2, HALF)),
            dma((2, NY)), dma((2, NY)),
            dma((2, NY)), dma((2, NY)),
            dma((2, NY)), dma((2,)),
            dma((NZ,)), dma((2,)),
            dma((2, NY)), dma((2, NY)),
            dma((2, NY)), dma((2, NY)),
            dma((2,)), dma((2,)),
            dma((2, NY)), dma((2, NY)),
            dma((NZ,)), dma,
            dma((NY,)), dma,
            dma((NY, 3)), dma((1,)),
        ],
        compiler_params=pltpu.CompilerParams(
            collective_id=0, has_side_effects=True, vmem_limit_bytes=56 * 1024 * 1024
        ),
        cost_estimate=pl.CostEstimate(flops=6_000_000_000, bytes_accessed=4_000_000, transcendentals=2_000_000),
        name="layer",
    )(
        hidden_rows[0], expert_ids[0], gate_weights[0], w_gate[0], w_up[0], w_down[0],
        query_latent.reshape(ROWS, LATENT), query_rope[0], cache_latent[0], cache_rope[0], offsets,
    )
    return passed[None], attended.reshape(1, TOKENS, HEADS, LATENT)


def solution(mesh):
    rows = P("section", "expert", None)
    heads = P("section", "expert", None, None)
    return jax.shard_map(
        per_device,
        mesh=mesh,
        in_specs=(rows, rows, rows, P("section", None, "expert"), P("section", None, "expert"), rows, heads, rows, rows, rows, P("section")),
        out_specs=(rows, heads),
        check_vma=False,
    )
```

time: 360 us -> 98.1 us (0.27); the launches traced: 356 us -> 97.8 us
  waiting for transfers between devices: 260 us -> 0 us
  Pallas kernels: 0 us -> 91.4 us
  starting transfers between devices: 33.7 us -> 0 us
  matrix products: 19.7 us -> 0 us
  local copies, waits for them, and re-layouts: 22.4 us -> 5.14 us
  between operations: 14.9 us -> 1.3 us
  other arithmetic: 5.07 us -> 0 us
    all_to_all x2 -> x0, waiting for transfers between devices: 178 us -> none  [the longest x1 90.3 us: per_device(): lax.all_to_all(expert_work(lax.all_to_all(outgoing, 'expert', split_axis=...]
    pallas_call x0 -> x1, Pallas kernels: none -> 91.4 us  [per_device(): pl.pallas_call(kernel, out_shape=(jax.ShapeDtypeStruct((TOKENS, WIDTH), b...]
    all_gather x2 -> x0, waiting for transfers between devices: 80.9 us -> none  [the longest x1 80.8 us: attention(): lat_piece = lax.all_gather(cache_lat, 'expert', axis=1, tiled=True)[0]]
    all_to_all x2 -> x0, starting transfers between devices: 29.4 us -> none  [the longest x1 19.7 us: per_device(): lax.all_to_all(outgoing, 'expert', split_axis=0, concat_axis=0, tiled=True)]
    dot_general x7 -> x0, matrix products: 19.7 us -> none  [the longest x1 6.02 us: attention(): jnp.einsum('thl,jl->thj', query_lat, lat_piece, preferred_element_type=jn...]
    all_gather x1 -> x0, local copies, waits for them, and re-layouts: 8.98 us -> none  [attention(): rot_piece = lax.all_gather(cache_rot, 'expert', axis=1, tiled=True)[0]]
    reshape x2 -> x0, local copies, waits for them, and re-layouts: 8.88 us -> none  [the longest x1 4.82 us: expert_work(): return product.reshape(received.shape)]
    ppermute x1 -> x0, starting transfers between devices: 4.3 us -> none  [shifted(): return lax.ppermute(block, axis, route)]
  transfers between devices with their start and end apart: 5 -> 0, of which waited for: 3 -> 0; matrix products, arithmetic and copies ran while one was open for 8% -> 0% of each run, Pallas kernels for 0% -> 0%
where the time goes in v1:
time: 98.1 us; the launch traced here: 97.8 us
  Pallas kernels  91.4 us (93%)
  local copies, waits for them, and re-layouts  5.14 us (5%)
  between operations  1.3 us (1%)
    pallas_call x1, Pallas kernels, per_device(): pl.pallas_call(kernel, out_shape=(jax.ShapeDtypeStruct((TOKENS, WIDTH), b...  91.4 us
    unnamed x6, local copies, waits for them, and re-layouts  3.79 us

profile of v1, /device:TPU:24, one launch (start us, length us, event | category | flops | bytes accessed | tf_op | source)
XLA Modules:
  0.0 97.8 jit_solution(8842779625814171911)
XLA Ops:
  1.3 0.0 copy-start
  1.3 0.7 copy-done
  2.0 0.0 copy-start.1
  2.0 0.7 copy.13.ids_ref
  2.6 0.0 copy-done.1
  2.6 0.7 copy.14.gate_ref
  3.3 91.4 %layer.1 = (bf16[8,3584]{1,0:T(8,128)(2,1)}, bf16[256,512]{1,0:T(8,128)(2,1)}) custom-call(bf16[8,3584]{1,0:T(8,128)(2,1)} %bitcast.21, s32[8,2]{1,0:T(8,128)} %copy.13.ids_ref, f32[8,2]{1,0:T(8,128)} %copy.14.gate_ref, bf16[3584,128]{1,0:T(8,128)(2,1)} %bitcast.16, bf16[3584,128]{1,0:T(8,128)(2,1)} %bitcast.17, bf16[128,3584]{1,0:T(8,128)(2,1)} %bitcast.18, ...), custom_call_target="tpu_custom_call" | custom-call | flops 6000000000 | bytes 4000000 | tf_op jit(solution)/shard_map/layer/pallas_call | solution.py:369
  94.7 1.4 %copy.18 = bf16[1,8,3584]{2,1,0:T(8,128)(2,1)} copy(bf16[1,8,3584]{2,1,0:T(8,128)(2,1)} %bitcast.13) | data formatting | bytes 114688
  96.1 1.7 %copy.19 = bf16[1,8,32,512]{3,2,1,0:T(8,128)(2,1)} copy(bf16[1,8,32,512]{3,2,1,0:T(8,128)(2,1)} %bitcast.12) | data formatting | bytes 524288
Async XLA Ops:
  1.3 0.7 copy-start
  2.0 0.7 copy-start.1

commit v2 on v1

--- a/solution.py
+++ b/solution.py
@@ -19,14 +19,9 @@
 WIDTH = 3584
 COLS = WIDTH // NY
 HALF = NZ // 2
-NEAR = NZ // 4
 scale_log2 = 192.0 ** (-0.5) * math.log2(math.e)
 masked_score = -1e30
 f32, bf16 = jnp.float32, jnp.bfloat16
-
-
-def slot_of(r):
-    return (r + NEAR) % NZ
 
 
 def kernel(
@@ -55,6 +50,9 @@
     def yplus(d):
         return lax.rem(y + (d % NY), NY)
 
+    side = lax.rem(z, 2)
+    outward = 2 * side - 1
+    pair = at(z - outward, y)
     next_sec = lax.rem(sec + 1, nsec)
     prev_sec = lax.rem(sec + nsec - 1, nsec)
     sends = []
@@ -114,8 +112,9 @@
         to = at(z, yplus(d))
         send(xs.at[yplus(d)], xs_recv.at[NY - d], send_d1.at[0, d], recv_d1.at[0], to)
         send(g_recv.at[0], g_recv.at[NY - d], send_d1.at[1, d], recv_d1.at[1], to)
-    send(kbuf.at[0, 0], kbuf.at[1, 0], send_ring.at[0, 0], recv_ring.at[0, 1], at(zplus(1), y))
-    send(kbuf.at[0, 0], kbuf.at[1, 2], send_ring.at[1, 0], recv_ring.at[1, 1], at(zplus(-1), y))
+    onward = 1 - 2 * c
+    following = at(lax.rem(z + onward + NZ, NZ), y)
+    send(kbuf.at[0, 0], kbuf.at[1, 0], send_ring.at[0, 0], recv_ring.at[1, 0], following)
     send(kbuf.at[0, 0], kbuf.at[0, 1], send_sib.at[0, 0], recv_sib.at[0, 0], (sec, sib))
     for d in (1, 3, 2):
         to = at(z, yplus(d))
@@ -128,35 +127,30 @@
     pick = jnp.where(jnp.transpose(gates)[: 8 * EXPERTS] != 0.0, 1.0, 0.0).astype(bf16)
     plane = xs_recv[...].astype(f32).reshape(NY * TOKENS, COLS).astype(bf16)
     packed[...] = jnp.dot(pick, plane, preferred_element_type=f32).reshape(EXPERTS, 8, COLS).astype(bf16)
-    mine = pltpu.make_async_copy(packed.at[lax.div(z, 2)], xall.at[0, 0, slot_of(0)], recv_d2.at[0])
+    mine = pltpu.make_async_copy(packed.at[lax.div(z, 2)], xall.at[0, 0, 0, 0], recv_d2)
     mine.start()
-    for r in sorted(range(1, NZ), key=lambda r: min(r, NZ - r)):
-        slot = slot_of(-r)
-        send(
-            packed.at[lax.div(zplus(r), 2)], xall.at[0, 0, slot], send_d2.at[r], recv_d2.at[slot // HALF], at(zplus(r), y)
-        )
+    for i in (4, 3, 5, 2, 6, 1, 7):
+        e = lax.rem(lax.div(z, 2) + i, EXPERTS)
+        delta = 2 * i - side
+        far = lax.div(delta, HALF)
+        u = delta + far * (NZ - 1 - 2 * delta)
+        send(packed.at[e], xall.at[0, 0, 0, u], send_d2.at[i], recv_d2, at(2 * e + far, y))
 
     def ring(s):
-        if s < HALF:
-            arrived(kbuf.at[s, 0], recv_ring.at[0, s])
-            arrived(kbuf.at[s, 2], recv_ring.at[1, s])
-            if s < HALF - 1:
-                send(kbuf.at[s, 0], kbuf.at[s + 1, 0], send_ring.at[0, s], recv_ring.at[0, s + 1], at(zplus(1), y))
-                send(kbuf.at[s, 2], kbuf.at[s + 1, 2], send_ring.at[1, s], recv_ring.at[1, s + 1], at(zplus(-1), y))
-            else:
-                low, high = pl.ds(0, KEYS // 2), pl.ds(KEYS // 2, KEYS // 2)
-                send(
-                    kbuf.at[s, 0, low], kbuf.at[0, 2, low], send_ring.at[0, s], recv_ring.at[0, s + 1], at(zplus(1), y)
-                )
-                send(
-                    kbuf.at[s, 2, high], kbuf.at[0, 2, high], send_ring.at[1, s], recv_ring.at[1, s + 1], at(zplus(-1), y)
-                )
-            send(kbuf.at[s, 0], kbuf.at[s, 1], send_sib.at[0, s], recv_sib.at[0, s], (sec, sib))
-            send(kbuf.at[s, 2], kbuf.at[s, 3], send_sib.at[1, s], recv_sib.at[1, s], (sec, sib))
+        if s == 0:
+            arrived(kbuf.at[0, 1], recv_sib.at[0, 0])
+            send(kbuf.at[0, 1], kbuf.at[1, 1], send_ring.at[0, 1], recv_ring.at[1, 1], following)
+        elif s < HALF:
+            for k in range(2):
+                arrived(kbuf.at[s, k], recv_ring.at[s, k])
+                if s < HALF - 1:
+                    send(kbuf.at[s, k], kbuf.at[s + 1, k], send_ring.at[s, k], recv_ring.at[s + 1, k], following)
+                elif k == 0:
+                    send(kbuf.at[s, 0], kbuf.at[0, 2], send_ring.at[s, 0], recv_ring.at[0, 0], following)
+                send(kbuf.at[s, k], kbuf.at[s, 2 + k], send_sib.at[s, k], recv_sib.at[s, k], (sec, sib))
         else:
-            arrived(kbuf.at[0, 2, pl.ds(0, KEYS // 2)], recv_ring.at[0, s])
-            arrived(kbuf.at[0, 2, pl.ds(KEYS // 2, KEYS // 2)], recv_ring.at[1, s])
-            send(kbuf.at[0, 2], kbuf.at[0, 3], send_sib.at[1, 0], recv_sib.at[1, 0], (sec, sib))
+            arrived(kbuf.at[0, 2], recv_ring.at[0, 0])
+            send(kbuf.at[0, 2], kbuf.at[0, 3], send_sib.at[0, 1], recv_sib.at[0, 1], (sec, sib))
 
     def spread_rope():
         keep = lax.broadcasted_iota(jnp.int32, (TOKENS, 128), 1) < ROPE
@@ -173,73 +167,75 @@
         lax.fori_loop(0, NY, one, 0)
 
     def attend(s, first):
-        arrived(kbuf.at[s, 1], recv_sib.at[0, s])
-        arrived(kbuf.at[s, 3], recv_sib.at[1, s])
+        if s == 0:
+            arrived(kbuf.at[0, 3], recv_sib.at[0, 1])
+        else:
+            for k in range(2):
+                arrived(kbuf.at[s, 2 + k], recv_sib.at[s, k])
         lanes = lax.broadcasted_iota(jnp.int32, (1, 1, 4 * KEYS), 2)
         block, inside = lanes // KEYS, lanes % KEYS
-        za, zb = (z, zplus(HALF)) if s == 0 else (zplus(-s), zplus(s))
-        zz = jnp.where(block < 2, za, zb)
-        cc = jnp.where(block % 2 == 0, c, 1 - c)
+        if s == 0:
+            zz = jnp.where(block < 2, z, zplus(HALF))
+            cc = jnp.where(block % 2 == 0, c, 1 - c)
+        else:
+            zz = jnp.where(block < 2, lax.rem(z - onward * s + NZ, NZ), lax.rem(z + onward * s + NZ, NZ))
+            cc = jnp.where((block == 0) | (block == 3), c, 1 - c)
         key_pos = ((zz * NY + y) * 2 + cc) * KEYS + inside
         kc = kbuf[s].reshape(4 * KEYS, KW)
         k_lat, k_rope = kc[:, :LATENT], kc[:, LATENT:]
         token_of = lax.broadcasted_iota(jnp.int32, (TOKENS, 1, 1), 0)
-
-        def one(d, carry):
-            owner = (z * NY + lax.rem(y + d, NY)) * 2 + c
-            position = offset_ref[0] + owner * TOKENS + token_of
+        contract = (((1,), (1,)), ((), ()))
+        scores = []
+        for d in range(NY):
+            score = lax.dot_general(ql[d], k_lat, contract, preferred_element_type=f32)
+            scores.append(score + lax.dot_general(qr[d], k_rope, contract, preferred_element_type=f32))
+        weights = []
+        for d in range(NY):
+            position = offset_ref[0] + ((z * NY + yplus(d)) * 2 + c) * TOKENS + token_of
             cap = jnp.where(key_pos <= position, jnp.inf, masked_score)
-            contract = (((1,), (1,)), ((), ()))
-            score = lax.dot_general(ql[d], k_lat, contract, preferred_element_type=f32)
-            score = score + lax.dot_general(qr[d], k_rope, contract, preferred_element_type=f32)
-            score = jnp.minimum(score.reshape(TOKENS, HEADS, 4 * KEYS), cap).reshape(ROWS, 4 * KEYS)
+            score = jnp.minimum(scores[d].reshape(TOKENS, HEADS, 4 * KEYS), cap).reshape(ROWS, 4 * KEYS)
             left, right = score[:, :128], score[:, 128:]
             top = jnp.max(jnp.maximum(left, right), axis=1, keepdims=True)
             if first:
-                new = jnp.broadcast_to(top, (ROWS, 128))
+                new, alpha = jnp.broadcast_to(top, (ROWS, 128)), None
             else:
                 old = m_ref[d]
                 new = jnp.maximum(old, top)
                 alpha = jnp.exp2((old - new) * scale_log2)
             left = jnp.exp2((left - new) * scale_log2)
             right = jnp.exp2((right - new) * scale_log2)
-            weights = jnp.concatenate([left.astype(bf16), right.astype(bf16)], axis=1)
-            value = jnp.dot(weights, k_lat, preferred_element_type=f32)
             m_ref[d] = new
-            if first:
-                l_ref[d] = left + right
-                acc[d] = value
-            else:
-                l_ref[d] = l_ref[d] * alpha + left + right
-                acc[d] = acc[d] * jnp.concatenate([alpha] * (LATENT // 128), axis=1) + value
-            return carry
-
-        lax.fori_loop(0, NY, one, 0)
+            l_ref[d] = left + right if first else l_ref[d] * alpha + left + right
+            weights.append((jnp.concatenate([left.astype(bf16), right.astype(bf16)], axis=1), alpha))
+        for d in range(NY):
+            weight, alpha = weights[d]
+            value = jnp.dot(weight, k_lat, preferred_element_type=f32)
+            acc[d] = value if first else acc[d] * jnp.concatenate([alpha] * (LATENT // 128), axis=1) + value
 
     def spread(half):
-        part = pl.ds(half * HALF, HALF)
-        arrived(xall.at[0, 0, part], recv_d2.at[half])
+        own = xall.at[0, 0, half]
+        arrived(own, recv_d2 if half == 0 else recv_d3.at[1, 0])
+        if half == 0:
+            send(own, xall.at[0, 0, 1], send_d3.at[1, 0], recv_d3.at[1, 0], pair)
+        for d in (1, 3, 2) if half == 0 else (1, 3):
+            send(own, xall.at[NY - d, 0, half], send_d3.at[half, d], recv_d3.at[half, NY - d], at(z, yplus(d)))
+        send(own, xall.at[0, 1, half], send_d3s.at[half, 0], recv_d3s.at[half, 0], (sec, sib))
+
+    def share_rows(half):
         for d in (1, 3, 2):
-            send(
-                xall.at[0, 0, part], xall.at[NY - d, 0, part], send_d3.at[half, d], recv_d3.at[half, NY - d],
-                at(z, yplus(d)),
-            )
-        send(xall.at[0, 0, part], xall.at[0, 1, part], send_d3s.at[half, 0], recv_d3s.at[half, 0], (sec, sib))
-
-    def share_rows(half):
-        part = pl.ds(half * HALF, HALF)
-        for d in (1, 3, 2):
-            arrived(xall.at[d, 0, part], recv_d3.at[half, d])
-            send(xall.at[d, 0, part], xall.at[d, 1, part], send_d3s.at[half, d], recv_d3s.at[half, d], (sec, sib))
+            got = xall.at[d, 0, half]
+            arrived(got, recv_d3.at[half, d])
+            if half == 0 and d == 2:
+                send(got, xall.at[d, 0, 1], send_d3.at[1, d], recv_d3.at[1, d], pair)
+            send(got, xall.at[d, 1, half], send_d3s.at[half, d], recv_d3s.at[half, d], (sec, sib))
 
     n_rows = HALF * 8
 
     def experts(half):
-        part = pl.ds(half * HALF, HALF)
         total = None
         for d in range(NY):
-            arrived(xall.at[d, 1, part], recv_d3s.at[half, d])
-            rows = xall[d, :, half * HALF : (half + 1) * HALF].astype(f32).reshape(2 * n_rows, COLS).astype(bf16)
+            arrived(xall.at[d, 1, half], recv_d3s.at[half, d])
+            rows = xall[d, :, half].astype(f32).reshape(2 * n_rows, COLS).astype(bf16)
             term = jnp.dot(rows, wgu[yplus(d)], preferred_element_type=f32)
             total = term if total is None else total + term
         gate, up = total[:, :128], total[:, 128:]
@@ -265,14 +261,14 @@
             arrived(cy_recv.at[half, d - 1], recv_c1.at[half, d])
             total = total + cy_recv[half, d - 1].astype(f32)
         csum[half] = total.astype(bf16)
-        for slot in range(half * HALF, (half + 1) * HALF):
-            r = (slot - NEAR) % NZ
-            block = csum.at[half, slot - half * HALF]
-            if r == 0:
-                back = pltpu.make_async_copy(block, ret.at[z], recv_c2)
-                back.start()
+        for u in reversed(range(HALF)):
+            block = csum.at[half, u]
+            if half == 0 and u == 0:
+                pltpu.make_async_copy(block, ret.at[z], recv_c2).start()
             else:
-                send(block, ret.at[z], send_c2.at[r], recv_c2, at(zplus(r), y))
+                distance = u if half == 0 else -1 - u
+                to = at(lax.rem(z + outward * distance + NZ, NZ), y)
+                send(block, ret.at[z], send_c2.at[half, u], recv_c2, to)
 
     def finish():
         arrived(ret, recv_c2)
@@ -316,40 +312,47 @@
             total = total + o_recv[d - 1].astype(f32) * factor
         out_ref[...] = total.astype(bf16)
 
+    def queries():
+        for d in (1, 3, 2):
+            arrived(ql.at[d], recv_q.at[0, d])
+            arrived(qraw.at[d], recv_q.at[1, d])
+        locals_[0].wait()
+        spread_rope()
+
+    def weights_here():
+        for copy in locals_[1:]:
+            copy.wait()
+
+    ring(0)
+    qraw[0] = qrope_ref[...]
     ring(1)
     ring(2)
     spread(0)
-    qraw[0] = qrope_ref[...]
     ring(3)
-    for d in (1, 3, 2):
-        arrived(ql.at[d], recv_q.at[0, d])
-        arrived(qraw.at[d], recv_q.at[1, d])
-    locals_[0].wait()
-    spread_rope()
+    spread(1)
+    queries()
+    attend(1, True)
     ring(4)
-    attend(1, True)
-    spread(1)
-    ring(5)
     share_rows(0)
     attend(2, False)
+    ring(5)
+    share_rows(1)
+    weights_here()
+    experts(0)
+    attend(3, False)
     ring(6)
-    for copy in locals_[1:]:
-        copy.wait()
-    experts(0)
+    experts(1)
+    combine(0)
+    attend(4, False)
+    combine(1)
     ring(7)
-    attend(3, False)
-    combine(0)
+    attend(5, False)
+    give_back(0)
     ring(8)
-    share_rows(1)
-    attend(4, False)
-    experts(1)
-    attend(5, False)
-    combine(1)
-    give_back(0)
     attend(6, False)
     attend(7, False)
+    give_back(1)
     attend(0, False)
-    give_back(1)
     give_out()
     finish()
     merge()
@@ -394,7 +397,7 @@
             pltpu.VMEM((NY, TOKENS, COLS), bf16),
             pltpu.VMEM((NY, TOKENS, 128), f32),
             pltpu.VMEM((EXPERTS, 8, COLS), bf16),
-            pltpu.VMEM((NY, 2, NZ, 8, COLS), bf16),
+            pltpu.VMEM((NY, 2, 2, HALF, 8, COLS), bf16),
             pltpu.VMEM((NY, COLS, 256), bf16),
             pltpu.VMEM((NY, 128, COLS), bf16),
             pltpu.VMEM((2, NY, HALF, 8, COLS), bf16),
@@ -406,17 +409,17 @@
             pltpu.VMEM((NZ, 8, COLS), bf16),
             pltpu.VMEM((NY, TOKENS, COLS), bf16),
             pltpu.VMEM((NY, TOKENS, COLS), bf16),
-            dma((2, HALF)), dma((2, HALF + 1)),
-            dma((2, HALF)), dma((2, HALF)),
+            dma((HALF, 2)), dma((HALF, 2)),
+            dma((HALF, 2)), dma((HALF, 2)),
             dma((2, NY)), dma((2, NY)),
             dma((2, NY)), dma((2, NY)),
             dma((2, NY)), dma((2,)),
-            dma((NZ,)), dma((2,)),
+            dma((HALF,)), dma,
             dma((2, NY)), dma((2, NY)),
             dma((2, NY)), dma((2, NY)),
             dma((2,)), dma((2,)),
             dma((2, NY)), dma((2, NY)),
-            dma((NZ,)), dma,
+            dma((2, HALF)), dma,
             dma((NY,)), dma,
             dma((NY, 3)), dma((1,)),
         ],

time: 98.1 us -> 83.4 us (0.85)
  the two profiles are of different devices: /device:TPU:24 before, /device:TPU:1 now
where the time goes in v2:
time: 83.4 us; the launch traced here: 83.1 us
  Pallas kernels  76.7 us (92%)
  local copies, waits for them, and re-layouts  5.14 us (6%)
  between operations  1.3 us (2%)
    pallas_call x1, Pallas kernels, per_device(): pl.pallas_call(kernel, out_shape=(jax.ShapeDtypeStruct((TOKENS, WIDTH), b...  76.7 us
    unnamed x6, local copies, waits for them, and re-layouts  3.79 us

profile of v2, /device:TPU:1, one launch (start us, length us, event | category | flops | bytes accessed | tf_op | source)
XLA Modules:
  0.0 83.1 jit_solution(3838094636720051579)
XLA Ops:
  1.3 0.0 copy-start
  1.3 0.7 copy-done
  2.0 0.0 copy-start.1
  2.0 0.7 copy.13.ids_ref
  2.6 0.0 copy-done.1
  2.6 0.7 copy.14.gate_ref
  3.3 76.7 %layer.1 = (bf16[8,3584]{1,0:T(8,128)(2,1)}, bf16[256,512]{1,0:T(8,128)(2,1)}) custom-call(bf16[8,3584]{1,0:T(8,128)(2,1)} %bitcast.21, s32[8,2]{1,0:T(8,128)} %copy.13.ids_ref, f32[8,2]{1,0:T(8,128)} %copy.14.gate_ref, bf16[3584,128]{1,0:T(8,128)(2,1)} %bitcast.16, bf16[3584,128]{1,0:T(8,128)(2,1)} %bitcast.17, bf16[128,3584]{1,0:T(8,128)(2,1)} %bitcast.18, ...), custom_call_target="tpu_custom_call" | custom-call | flops 6000000000 | bytes 4000000 | tf_op jit(solution)/shard_map/layer/pallas_call | solution.py:372
  80.0 1.4 %copy.18 = bf16[1,8,3584]{2,1,0:T(8,128)(2,1)} copy(bf16[1,8,3584]{2,1,0:T(8,128)(2,1)} %bitcast.13) | data formatting | bytes 114688
  81.4 1.7 %copy.19 = bf16[1,8,32,512]{3,2,1,0:T(8,128)(2,1)} copy(bf16[1,8,32,512]{3,2,1,0:T(8,128)(2,1)} %bitcast.12) | data formatting | bytes 524288
Async XLA Ops:
  1.3 0.7 copy-start
  2.0 0.7 copy-start.1

commit v3 on v2

v3 whole, which is shorter than its diff:
```python
import functools
import math

import jax
import jax.numpy as jnp
from jax import lax
from jax.experimental import pallas as pl
from jax.experimental.pallas import tpu as pltpu
from jax.sharding import PartitionSpec as P

MESH = pl.DeviceIdType.MESH
EXPERTS = 8
NZ, NY = 16, 4
TOKENS, HEADS = 8, 32
ROWS = TOKENS * HEADS
LATENT, ROPE = 512, 64
KEYS = 64
KW = LATENT + 128
WIDTH = 3584
COLS = WIDTH // NY
HALF = NZ // 2
QUART = HALF // 2
PARTS = 4
scale_log2 = 192.0 ** (-0.5) * math.log2(math.e)
masked_score = -1e30
f32, bf16 = jnp.float32, jnp.bfloat16


def kernel(
    x_ref, ids_ref, gate_ref, wg_ref, wu_ref, wd_ref, q_ref, qrope_ref, klat_ref, krope_ref, offset_ref,
    passed_ref, out_ref,
    kbuf, ql, qraw, qr, rel, acc, m_ref, l_ref, o_far, o_far_recv, o_near, o_recv, ls_far, ls_far_recv, ls_near, ls_recv,
    xs, xs_recv, g_recv, packed, hid, xall, wgu, wd, csib_send, csib_recv, own_sum,
    cy_send, cy_recv, csum, pair_recv, ret, fin, fin_recv,
    send_ring, recv_ring, send_sib, recv_sib, send_q, recv_q, send_o, recv_o,
    send_d1, recv_d1, send_d2, recv_d2, send_d3, recv_d3, send_d3s, recv_d3s,
    send_c0, recv_c0, send_c1, recv_c1, send_pair, recv_pair, send_c2, recv_c2, send_fin, recv_fin, sem_w, sem_l,
):
    sec = lax.axis_index("section")
    nsec = lax.axis_size("section")
    me = lax.axis_index("expert")
    c = lax.rem(me, 2)
    y = lax.rem(lax.div(me, 2), NY)
    z = lax.div(me, 2 * NY)
    sib = me + 1 - 2 * c

    def at(zz, yy):
        return (sec, (zz * NY + yy) * 2 + c)

    def zplus(r):
        return lax.rem(z + (r % NZ), NZ)

    def yplus(d):
        return lax.rem(y + (d % NY), NY)

    side = lax.rem(z, 2)
    outward = 2 * side - 1
    pair = at(z - outward, y)
    next_sec = lax.rem(sec + 1, nsec)
    prev_sec = lax.rem(sec + nsec - 1, nsec)
    sends = []

    def send(src, dst, ssem, rsem, device):
        copy = pltpu.make_async_remote_copy(
            src_ref=src, dst_ref=dst, send_sem=ssem, recv_sem=rsem, device_id=device, device_id_type=MESH
        )
        copy.start()
        sends.append(copy)

    def arrived(ref, sem):
        pltpu.make_async_copy(ref, ref, sem).wait()

    barrier = pltpu.get_barrier_semaphore()

    def greet(device):
        pl.semaphore_signal(barrier, inc=1, device_id=device, device_id_type=MESH)

    greet((sec, sib))
    for d in range(1, NY):
        greet(at(z, yplus(d)))
    for r in range(1, NZ):
        greet(at(zplus(r), y))
    for d in range(NY):
        greet((prev_sec, (z * NY + d) * 2 + c))

    locals_ = [pltpu.make_async_copy(q_ref, ql.at[0], sem_l.at[0])]
    for k in range(NY):
        rows = pl.ds(k * COLS, COLS)
        locals_.append(pltpu.make_async_copy(wg_ref.at[rows, :], wgu.at[k, :, pl.ds(0, 128)], sem_w.at[k, 0]))
        locals_.append(pltpu.make_async_copy(wu_ref.at[rows, :], wgu.at[k, :, pl.ds(128, 128)], sem_w.at[k, 1]))
        locals_.append(pltpu.make_async_copy(wd_ref.at[:, rows], wd.at[k], sem_w.at[k, 2]))
    for copy in locals_:
        copy.start()

    kbuf[0, 0, :, :LATENT] = klat_ref[...]
    kbuf[0, 0, :, LATENT:] = jnp.concatenate([krope_ref[...], jnp.zeros((KEYS, 128 - ROPE), bf16)], axis=1)

    lane = lax.broadcasted_iota(jnp.int32, (TOKENS, 128), 1)
    token = lax.broadcasted_iota(jnp.int32, (TOKENS, 128), 0)

    diagonal = lax.broadcasted_iota(jnp.int32, (TOKENS, TOKENS), 0) == lax.broadcasted_iota(jnp.int32, (TOKENS, TOKENS), 1)

    def upright(row):
        return jnp.sum(jnp.where(diagonal, jnp.broadcast_to(row, (TOKENS, TOKENS)), 0.0), axis=1, keepdims=True)

    named_first = upright(ids_ref[0:1, :].astype(f32)).astype(jnp.int32)
    named_second = upright(ids_ref[1:2, :].astype(f32)).astype(jnp.int32)
    share_first, share_second = upright(gate_ref[0:1, :]), upright(gate_ref[1:2, :])

    def slots(lane_e, lane_rank):
        first, second = named_first == lane_e, named_second == lane_e
        hit = jnp.where(first | second, 1, 0)
        rank = jnp.zeros((TOKENS, 128), jnp.int32)
        for t in range(TOKENS - 1):
            rank = rank + jnp.where(token > t, hit[t : t + 1, :], 0)
        share = jnp.where(first, share_first, share_second)
        return jnp.where((hit == 1) & (rank == lane_rank), share, 0.0)

    mine = jnp.where(slots(lane >> 1, lane & 1) != 0.0, 1.0, 0.0)
    pick = jnp.transpose(jnp.concatenate([mine, jnp.zeros((TOKENS, 128), f32)], axis=0))[: 2 * EXPERTS].astype(bf16)
    rows_in = x_ref[...].astype(f32)
    rows_in = jnp.concatenate([rows_in, jnp.zeros_like(rows_in)], axis=0).astype(bf16)
    sorted_rows = jnp.dot(pick, rows_in, preferred_element_type=f32).astype(bf16)
    for k in range(NY):
        xs[k] = sorted_rows[:, k * COLS : (k + 1) * COLS]
    xs_recv[0] = xs[y]
    g_recv[0] = jnp.where(((lane >> 1) & 3) == y, slots(lane >> 3, lane & 1), 0.0)
    to_row = lax.broadcasted_iota(jnp.int32, (8 * EXPERTS, 8 * EXPERTS), 0)
    from_row = lax.broadcasted_iota(jnp.int32, (8 * EXPERTS, 8 * EXPERTS), 1)
    same = ((to_row >> 3) == ((from_row >> 1) & 7)) & ((to_row & 1) == (from_row & 1))
    order = jnp.where(same & (((to_row >> 1) & 3) == (((from_row >> 4) + y) & 3)), 1.0, 0.0).astype(bf16)

    pl.semaphore_wait(barrier, 1 + (NY - 1) + (NZ - 1) + NY)

    for d in range(1, NY):
        to = at(z, yplus(d))
        send(xs.at[yplus(d)], xs_recv.at[NY - d], send_d1.at[0, d], recv_d1.at[0], to)
        send(g_recv.at[0], g_recv.at[NY - d], send_d1.at[1, d], recv_d1.at[1], to)
    onward = 1 - 2 * c
    following = at(lax.rem(z + onward + NZ, NZ), y)
    send(kbuf.at[0, 0], kbuf.at[1, 0], send_ring.at[0, 0], recv_ring.at[1, 0], following)
    send(kbuf.at[0, 0], kbuf.at[0, 1], send_sib.at[0, 0], recv_sib.at[0, 0], (sec, sib))
    for d in (1, 3):
        to = at(z, yplus(d))
        send(q_ref, ql.at[NY - d], send_q.at[0, d], recv_q.at[0, NY - d], to)
        send(qrope_ref, qraw.at[NY - d], send_q.at[1, d], recv_q.at[1, NY - d], to)

    def dispatch():
        arrived(xs_recv.at[pl.ds(1, NY - 1)], recv_d1.at[0])
        rows = jnp.dot(order, xs_recv[...].reshape(8 * EXPERTS, COLS), preferred_element_type=f32)
        packed[...] = rows.reshape(EXPERTS, 8, COLS).astype(bf16)
        pltpu.make_async_copy(packed.at[lax.div(z, 2)], xall.at[0, 0, 0, 0], recv_d2.at[0]).start()
        for i in (1, 7, 2, 6, 3, 5, 4):
            e = lax.rem(lax.div(z, 2) + i, EXPERTS)
            delta = 2 * i - side
            far = lax.div(delta, HALF)
            u = delta + far * (NZ - 1 - 2 * delta)
            part = lax.div(u, QUART)
            slot = xall.at[0, 0, part, lax.rem(u, QUART)]
            send(packed.at[e], slot, send_d2.at[i], recv_d2.at[part], at(2 * e + far, y))

    def gates():
        return g_recv[...].reshape(NY * TOKENS, 128)[:, : 8 * EXPERTS]

    def keep_rows():
        arrived(g_recv.at[pl.ds(1, NY - 1)], recv_d1.at[1])
        named = jnp.where(gates() != 0.0, 0.5, 0.0).astype(bf16)
        rows = packed[...].astype(f32).reshape(8 * EXPERTS, COLS).astype(bf16)
        hid[...] = jnp.dot(named, rows, preferred_element_type=f32)

    def ring(s):
        if s == 0:
            arrived(kbuf.at[0, 1], recv_sib.at[0, 0])
            send(kbuf.at[0, 1], kbuf.at[1, 1], send_ring.at[0, 1], recv_ring.at[1, 1], following)
        elif s < HALF:
            for k in range(2):
                arrived(kbuf.at[s, k], recv_ring.at[s, k])
                if s < HALF - 1:
                    send(kbuf.at[s, k], kbuf.at[s + 1, k], send_ring.at[s, k], recv_ring.at[s + 1, k], following)
                elif k == 0:
                    send(kbuf.at[s, 0], kbuf.at[0, 2], send_ring.at[s, 0], recv_ring.at[0, 0], following)
                send(kbuf.at[s, k], kbuf.at[s, 2 + k], send_sib.at[s, k], recv_sib.at[s, k], (sec, sib))
        else:
            arrived(kbuf.at[0, 2], recv_ring.at[0, 0])
            send(kbuf.at[0, 2], kbuf.at[0, 3], send_sib.at[0, 1], recv_sib.at[0, 1], (sec, sib))

    def spread_rope():
        keep = lax.broadcasted_iota(jnp.int32, (TOKENS, 128), 1) < ROPE

        def one(d, carry):
            for h in range(HEADS):
                pair = qraw[d, :, (h // 2) * 128 : (h // 2 + 1) * 128].astype(f32)
                if h % 2:
                    pair = pltpu.roll(pair, ROPE, 1)
                rel[pl.ds(h, TOKENS, stride=HEADS), :] = jnp.where(keep, pair, 0.0)
            qr[d] = rel[...].astype(bf16)
            return carry

        lax.fori_loop(0, NY, one, 0)

    def attend(s, first):
        if s == 0:
            arrived(kbuf.at[0, 3], recv_sib.at[0, 1])
        else:
            for k in range(2):
                arrived(kbuf.at[s, 2 + k], recv_sib.at[s, k])
        lanes = lax.broadcasted_iota(jnp.int32, (1, 1, 4 * KEYS), 2)
        block, inside = lanes // KEYS, lanes % KEYS
        if s == 0:
            zz = jnp.where(block < 2, z, zplus(HALF))
            cc = jnp.where(block % 2 == 0, c, 1 - c)
        else:
            zz = jnp.where(block < 2, lax.rem(z - onward * s + NZ, NZ), lax.rem(z + onward * s + NZ, NZ))
            cc = jnp.where((block == 0) | (block == 3), c, 1 - c)
        key_pos = ((zz * NY + y) * 2 + cc) * KEYS + inside
        kc = kbuf[s].reshape(4 * KEYS, KW)
        k_lat, k_rope = kc[:, :LATENT], kc[:, LATENT:]
        token_of = lax.broadcasted_iota(jnp.int32, (TOKENS, 1, 1), 0)
        contract = (((1,), (1,)), ((), ()))
        scores = []
        for d in range(NY):
            score = lax.dot_general(ql[d], k_lat, contract, preferred_element_type=f32)
            scores.append(score + lax.dot_general(qr[d], k_rope, contract, preferred_element_type=f32))
        weights = []
        for d in range(NY):
            position = offset_ref[0] + ((z * NY + yplus(d)) * 2 + c) * TOKENS + token_of
            cap = jnp.where(key_pos <= position, jnp.inf, masked_score)
            score = jnp.minimum(scores[d].reshape(TOKENS, HEADS, 4 * KEYS), cap).reshape(ROWS, 4 * KEYS)
            left, right = score[:, :128], score[:, 128:]
            top = jnp.max(jnp.maximum(left, right), axis=1, keepdims=True)
            if first:
                new, alpha = jnp.broadcast_to(top, (ROWS, 128)), None
            else:
                old = m_ref[d]
                new = jnp.maximum(old, top)
                alpha = jnp.exp2((old - new) * scale_log2)
            left = jnp.exp2((left - new) * scale_log2)
            right = jnp.exp2((right - new) * scale_log2)
            m_ref[d] = new
            l_ref[d] = left + right if first else l_ref[d] * alpha + left + right
            weights.append((jnp.concatenate([left.astype(bf16), right.astype(bf16)], axis=1), alpha))
        for d in range(NY):
            weight, alpha = weights[d]
            value = jnp.dot(weight, k_lat, preferred_element_type=f32)
            acc[d] = value if first else acc[d] * jnp.concatenate([alpha] * (LATENT // 128), axis=1) + value

    def spread(p):
        own = xall.at[0, 0, p]
        arrived(own, recv_d2.at[p] if p < 2 else recv_d3.at[p, 0])
        if p < 2:
            send(own, xall.at[0, 0, p + 2], send_d3.at[p + 2, 0], recv_d3.at[p + 2, 0], pair)
        for d in (2, 1, 3) if p < 2 else (1, 3):
            send(own, xall.at[NY - d, 0, p], send_d3.at[p, d], recv_d3.at[p, NY - d], at(z, yplus(d)))
        send(own, xall.at[0, 1, p], send_d3s.at[p, 0], recv_d3s.at[p, 0], (sec, sib))

    def share_rows(p):
        for d in (1, 3, 2):
            arrived(xall.at[d, 0, p], recv_d3.at[p, d])
            if d == 2 and p < 2:
                send(xall.at[2, 0, p], xall.at[2, 0, p + 2], send_d3.at[p + 2, 2], recv_d3.at[p + 2, 2], pair)
            send(xall.at[d, 0, p], xall.at[d, 1, p], send_d3s.at[p, d], recv_d3s.at[p, d], (sec, sib))

    n_rows = QUART * 8

    def experts(p):
        total = None
        for d in (0, 1, 3, 2):
            arrived(xall.at[d, 1, p], recv_d3s.at[p, d])
            rows = xall[d, :, p].astype(f32).reshape(2 * n_rows, COLS).astype(bf16)
            term = jnp.dot(rows, wgu[yplus(d)], preferred_element_type=f32)
            total = term if total is None else total + term
        gate, up = total[:, :128], total[:, 128:]
        active = (gate / (1.0 + jnp.exp(-gate)) * up).astype(bf16)
        for d in range(NY):
            piece = jnp.dot(active, wd[yplus(d)], preferred_element_type=f32).reshape(2, QUART, 8, COLS)
            own_sum[p, d] = piece[0]
            csib_send[p, d] = piece[1].astype(bf16)
        send(csib_send.at[p], csib_recv.at[p], send_c0.at[p], recv_c0.at[p], (sec, sib))

    def chunk(p, d):
        return own_sum[p, d] + csib_recv[p, d].astype(f32)

    def combine(p):
        arrived(csib_recv.at[p], recv_c0.at[p])
        if p >= 2:
            cy_send[p, 1] = chunk(p, 2).astype(bf16)
            send(cy_send.at[p, 1], pair_recv.at[0, p - 2], send_pair.at[0, p - 2], recv_pair.at[0, p - 2], pair)
        for d in (1, 3):
            cy_send[p, d - 1] = chunk(p, d).astype(bf16)
            send(
                cy_send.at[p, d - 1], cy_recv.at[p, NY - d - 1], send_c1.at[p, d], recv_c1.at[p, NY - d], at(z, yplus(d))
            )

    def combine_far(p):
        arrived(pair_recv.at[0, p], recv_pair.at[0, p])
        cy_send[p, 1] = (chunk(p, 2) + pair_recv[0, p].astype(f32)).astype(bf16)
        send(cy_send.at[p, 1], cy_recv.at[p, 1], send_c1.at[p, 2], recv_c1.at[p, 2], at(z, yplus(2)))

    def give_back(p):
        total = chunk(p, 0)
        for d in (1, 3, 2) if p < 2 else (1, 3):
            arrived(cy_recv.at[p, d - 1], recv_c1.at[p, d])
            total = total + cy_recv[p, d - 1].astype(f32)
        if p >= 2:
            csum[p] = total.astype(bf16)
            send(csum.at[p], pair_recv.at[1, p - 2], send_pair.at[1, p - 2], recv_pair.at[1, p - 2], pair)
            return
        arrived(pair_recv.at[1, p], recv_pair.at[1, p])
        csum[p] = (total + pair_recv[1, p].astype(f32)).astype(bf16)
        for k in reversed(range(QUART)):
            u = k + QUART * p
            home = ret.at[lax.div(z, 2)]
            if u == 0:
                pltpu.make_async_copy(csum.at[p, k], home, recv_c2).start()
            else:
                to = at(lax.rem(z + outward * u + NZ, NZ), y)
                send(csum.at[p, k], home, send_c2.at[p, k], recv_c2, to)

    def finish():
        arrived(ret, recv_c2)
        rows = ret[...].astype(f32).reshape(8 * EXPERTS, COLS).astype(bf16)
        weights = gates()
        high = weights.astype(bf16)
        low = (weights - high.astype(f32)).astype(bf16)
        mixture = jnp.dot(high, rows, preferred_element_type=f32) + jnp.dot(low, rows, preferred_element_type=f32)
        result = (hid[...] + mixture).reshape(NY, TOKENS, COLS)
        fin[...] = result.astype(bf16)
        for d in range(NY):
            to = (next_sec, (z * NY + yplus(d)) * 2 + c)
            send(fin.at[d], fin_recv.at[y], send_fin.at[d], recv_fin, to)

    def close(d):
        total = jnp.sum(l_ref[d], axis=1, keepdims=True)
        level = m_ref[d] * scale_log2 + jnp.log2(total)
        return level, acc[d] * (1.0 / total)

    def wide(factor):
        return jnp.concatenate([factor] * (LATENT // 128), axis=1)

    def column(ref, start, size):
        return jnp.transpose(jnp.broadcast_to(ref[0:1, start : start + size], (128, size)))

    half_rows = ROWS // 2

    def give_out_far():
        level, value = close(2)
        o_far[...] = value.astype(bf16).reshape(2, half_rows, LATENT)
        ls_far[...] = jnp.transpose(level)[:8, :]
        for q in range(2):
            to = at(z, yplus(1 + 2 * q))
            send(o_far.at[q], o_far_recv.at[q], send_o.at[q, 0], recv_o.at[q, 0], to)
            send(ls_far, ls_far_recv.at[q], send_o.at[q, 1], recv_o.at[q, 1], to)
        for q in range(2):
            to = at(z, yplus(1 + 2 * q))
            level, value = close(1 + 2 * q)
            m_ref[1 + 2 * q] = level
            acc[1 + 2 * q] = value
            rest = slice((1 - q) * half_rows, (2 - q) * half_rows)
            o_near[q, 1 - q] = value[rest].astype(bf16)
            send(o_near.at[q, 1 - q], o_recv.at[q, 1 - q], send_o.at[q, 2], recv_o.at[q, 2], to)

    def give_out_near():
        for q in range(2):
            to = at(z, yplus(1 + 2 * q))
            arrived(o_far_recv.at[q], recv_o.at[q, 0])
            arrived(ls_far_recv.at[q], recv_o.at[q, 1])
            rows = slice(q * half_rows, (q + 1) * half_rows)
            here, there = m_ref[1 + 2 * q, rows], column(ls_far_recv.at[q], q * half_rows, half_rows)
            best = jnp.maximum(here, there)
            here, there = jnp.exp2(here - best), jnp.exp2(there - best)
            norm = 1.0 / (here + there)
            value = acc[1 + 2 * q, rows] * wide(here * norm) + o_far_recv[q].astype(f32) * wide(there * norm)
            o_near[q, q] = value.astype(bf16)
            m_ref[1 + 2 * q, rows] = best + jnp.log2(here + there)
            ls_near[q] = jnp.transpose(m_ref[1 + 2 * q])[:8, :]
            send(o_near.at[q, q], o_recv.at[q, q], send_o.at[q, 3], recv_o.at[q, 3], to)
            send(ls_near.at[q], ls_recv.at[q], send_o.at[q, 4], recv_o.at[q, 4], to)

    def merge():
        level, value = close(0)
        levels, values = [level], [value]
        for q in range(2):
            arrived(o_recv.at[q, 1 - q], recv_o.at[q, 2])
            arrived(o_recv.at[q, q], recv_o.at[q, 3])
            arrived(ls_recv.at[q], recv_o.at[q, 4])
            levels.append(column(ls_recv.at[q], 0, ROWS))
            values.append(o_recv[q].reshape(ROWS, LATENT).astype(f32))
        best = functools.reduce(jnp.maximum, levels)
        shares = [jnp.exp2(one - best) for one in levels]
        norm = 1.0 / functools.reduce(jnp.add, shares)
        out_ref[...] = sum(one * wide(share * norm) for one, share in zip(values, shares)).astype(bf16)

    def queries_on():
        for d in (1, 3):
            q = d // 2
            rows = pl.ds(q * half_rows, half_rows)
            to = at(z, yplus(NY - d))
            arrived(ql.at[d], recv_q.at[0, d])
            send(ql.at[d, rows], ql.at[2, rows], send_q.at[2, q], recv_q.at[2, q], to)
            arrived(qraw.at[d], recv_q.at[1, d])
            if q == 0:
                send(qraw.at[d], qraw.at[2], send_q.at[1, 2], recv_q.at[1, 2], to)

    def queries():
        for q in range(2):
            arrived(ql.at[2, pl.ds(q * half_rows, half_rows)], recv_q.at[2, q])
        arrived(qraw.at[2], recv_q.at[1, 2])
        locals_[0].wait()
        spread_rope()

    def weights_here():
        for copy in locals_[1:]:
            copy.wait()

    dispatch()
    ring(0)
    qraw[0] = qrope_ref[...]
    ring(1)
    spread(0)
    keep_rows()
    queries_on()
    ring(2)
    spread(2)
    spread(1)
    ring(3)
    share_rows(0)
    spread(3)
    share_rows(2)
    weights_here()
    ring(4)
    experts(0)
    share_rows(1)
    experts(2)
    queries()
    ring(5)
    share_rows(3)
    combine(2)
    experts(1)
    combine(0)
    attend(1, True)
    experts(3)
    ring(6)
    attend(2, False)
    combine(3)
    combine(1)
    combine_far(0)
    give_back(2)
    ring(7)
    attend(3, False)
    combine_far(1)
    attend(4, False)
    give_back(3)
    ring(8)
    attend(5, False)
    give_back(0)
    attend(6, False)
    attend(7, False)
    give_back(1)
    attend(0, False)
    give_out_far()
    give_out_near()
    finish()
    merge()
    arrived(fin_recv, recv_fin)
    for k in range(NY):
        passed_ref[:, k * COLS : (k + 1) * COLS] = fin_recv[k]
    for copy in sends:
        copy.wait_send()


def per_device(
    hidden_rows, expert_ids, gate_weights, w_gate, w_up, w_down, query_latent, query_rope, cache_latent, cache_rope, offsets
):
    vmem = pl.BlockSpec(memory_space=pltpu.VMEM)
    anywhere = pl.BlockSpec(memory_space=pl.ANY)
    dma = pltpu.SemaphoreType.DMA
    passed, attended = pl.pallas_call(
        kernel,
        out_shape=(
            jax.ShapeDtypeStruct((TOKENS, WIDTH), bf16),
            jax.ShapeDtypeStruct((ROWS, LATENT), bf16),
        ),
        in_specs=[
            vmem, vmem, vmem, anywhere, anywhere, anywhere, anywhere, vmem, vmem, vmem,
            pl.BlockSpec(memory_space=pltpu.SMEM),
        ],
        out_specs=(vmem, vmem),
        scratch_shapes=[
            pltpu.VMEM((HALF, 4, KEYS, KW), bf16),
            pltpu.VMEM((NY, ROWS, LATENT), bf16),
            pltpu.VMEM((NY, TOKENS, HEADS * ROPE), bf16),
            pltpu.VMEM((NY, ROWS, 128), bf16),
            pltpu.VMEM((ROWS, 128), f32),
            pltpu.VMEM((NY, ROWS, LATENT), f32),
            pltpu.VMEM((NY, ROWS, 128), f32),
            pltpu.VMEM((NY, ROWS, 128), f32),
            pltpu.VMEM((2, ROWS // 2, LATENT), bf16),
            pltpu.VMEM((2, ROWS // 2, LATENT), bf16),
            pltpu.VMEM((2, 2, ROWS // 2, LATENT), bf16),
            pltpu.VMEM((2, 2, ROWS // 2, LATENT), bf16),
            pltpu.VMEM((8, ROWS), f32),
            pltpu.VMEM((2, 8, ROWS), f32),
            pltpu.VMEM((2, 8, ROWS), f32),
            pltpu.VMEM((2, 8, ROWS), f32),
            pltpu.VMEM((NY, 2 * EXPERTS, COLS), bf16),
            pltpu.VMEM((NY, 2 * EXPERTS, COLS), bf16),
            pltpu.VMEM((NY, TOKENS, 128), f32),
            pltpu.VMEM((EXPERTS, 8, COLS), bf16),
            pltpu.VMEM((NY * TOKENS, COLS), f32),
            pltpu.VMEM((NY, 2, PARTS, QUART, 8, COLS), bf16),
            pltpu.VMEM((NY, COLS, 256), bf16),
            pltpu.VMEM((NY, 128, COLS), bf16),
            pltpu.VMEM((PARTS, NY, QUART, 8, COLS), bf16),
            pltpu.VMEM((PARTS, NY, QUART, 8, COLS), bf16),
            pltpu.VMEM((PARTS, NY, QUART, 8, COLS), f32),
            pltpu.VMEM((PARTS, NY - 1, QUART, 8, COLS), bf16),
            pltpu.VMEM((PARTS, NY - 1, QUART, 8, COLS), bf16),
            pltpu.VMEM((PARTS, QUART, 8, COLS), bf16),
            pltpu.VMEM((2, 2, QUART, 8, COLS), bf16),
            pltpu.VMEM((EXPERTS, 8, COLS), bf16),
            pltpu.VMEM((NY, TOKENS, COLS), bf16),
            pltpu.VMEM((NY, TOKENS, COLS), bf16),
            dma((HALF, 2)), dma((HALF, 2)),
            dma((HALF, 2)), dma((HALF, 2)),
            dma((3, NY)), dma((3, NY)),
            dma((2, 5)), dma((2, 5)),
            dma((2, NY)), dma((2,)),
            dma((HALF,)), dma((2,)),
            dma((PARTS, NY)), dma((PARTS, NY)),
            dma((PARTS, NY)), dma((PARTS, NY)),
            dma((PARTS,)), dma((PARTS,)),
            dma((PARTS, NY)), dma((PARTS, NY)),
            dma((2, 2)), dma((2, 2)),
            dma((2, QUART)), dma,
            dma((NY,)), dma,
            dma((NY, 3)), dma((1,)),
        ],
        compiler_params=pltpu.CompilerParams(
            collective_id=0, has_side_effects=True, vmem_limit_bytes=56 * 1024 * 1024
        ),
        cost_estimate=pl.CostEstimate(flops=6_000_000_000, bytes_accessed=4_000_000, transcendentals=2_000_000),
        name="layer",
    )(
        hidden_rows[0], expert_ids[0].T, gate_weights[0].T, w_gate[0], w_up[0], w_down[0],
        query_latent.reshape(ROWS, LATENT), query_rope[0], cache_latent[0], cache_rope[0], offsets,
    )
    return passed[None], attended.reshape(1, TOKENS, HEADS, LATENT)


def solution(mesh):
    rows = P("section", "expert", None)
    heads = P("section", "expert", None, None)
    return jax.shard_map(
        per_device,
        mesh=mesh,
        in_specs=(rows, rows, rows, P("section", None, "expert"), P("section", None, "expert"), rows, heads, rows, rows, rows, P("section")),
        out_specs=(rows, heads),
        check_vma=False,
    )
```

time: 83.4 us -> 78.1 us (0.936)
  the two profiles are of different devices: /device:TPU:1 before, /device:TPU:24 now
where the time goes in v3:
time: 78.1 us; the launch traced here: 77.9 us
  Pallas kernels  73.5 us (94%)
  local copies, waits for them, and re-layouts  3.11 us (4%)
  between operations  1.29 us (2%)
    pallas_call x1, Pallas kernels, per_device(): pl.pallas_call(kernel, out_shape=(jax.ShapeDtypeStruct((TOKENS, WIDTH), b...  73.5 us
    unnamed x2, local copies, waits for them, and re-layouts  3.11 us

profile of v3, /device:TPU:24, one launch (start us, length us, event | category | flops | bytes accessed | tf_op | source)
XLA Modules:
  0.0 77.9 jit_solution(3710556977206753129)
XLA Ops:
  1.3 73.5 %layer.1 = (bf16[8,3584]{1,0:T(8,128)(2,1)}, bf16[256,512]{1,0:T(8,128)(2,1)}) custom-call(bf16[8,3584]{1,0:T(8,128)(2,1)} %bitcast.23, s32[2,8]{1,0:T(2,128)} %bitcast.26, f32[2,8]{1,0:T(2,128)} %bitcast.27, bf16[3584,128]{1,0:T(8,128)(2,1)} %bitcast.18, bf16[3584,128]{1,0:T(8,128)(2,1)} %bitcast.19, bf16[128,3584]{1,0:T(8,128)(2,1)} %bitcast.20, ...), custom_call_target="tpu_custom_call" | custom-call | flops 6000000000 | bytes 4000000 | tf_op jit(solution)/shard_map/layer/pallas_call | solution.py:477
  74.8 1.4 %copy.16 = bf16[1,8,3584]{2,1,0:T(8,128)(2,1)} copy(bf16[1,8,3584]{2,1,0:T(8,128)(2,1)} %bitcast.17) | data formatting | bytes 114688
  76.2 1.7 %copy.17 = bf16[1,8,32,512]{3,2,1,0:T(8,128)(2,1)} copy(bf16[1,8,32,512]{3,2,1,0:T(8,128)(2,1)} %bitcast.16) | data formatting | bytes 524288

commit v4 on v3

--- a/solution.py
+++ b/solution.py
@@ -27,7 +27,7 @@
 
 
 def kernel(
-    x_ref, ids_ref, gate_ref, wg_ref, wu_ref, wd_ref, q_ref, qrope_ref, klat_ref, krope_ref, offset_ref,
+    x_hbm, ids_hbm, gate_hbm, wg_ref, wu_ref, wd_ref, q_ref, qrope_hbm, klat_hbm, krope_hbm, offset_ref,
     passed_ref, out_ref,
     kbuf, ql, qraw, qr, rel, acc, m_ref, l_ref, o_far, o_far_recv, o_near, o_recv, ls_far, ls_far_recv, ls_near, ls_recv,
     xs, xs_recv, g_recv, packed, hid, xall, wgu, wd, csib_send, csib_recv, own_sum,
@@ -35,6 +35,7 @@
     send_ring, recv_ring, send_sib, recv_sib, send_q, recv_q, send_o, recv_o,
     send_d1, recv_d1, send_d2, recv_d2, send_d3, recv_d3, send_d3s, recv_d3s,
     send_c0, recv_c0, send_c1, recv_c1, send_pair, recv_pair, send_c2, recv_c2, send_fin, recv_fin, sem_w, sem_l,
+    x_ref, ids_ref, gate_ref, qrope_ref, klat_ref, krope_ref, sem_in,
 ):
     sec = lax.axis_index("section")
     nsec = lax.axis_size("section")
@@ -83,6 +84,13 @@
     for d in range(NY):
         greet((prev_sec, (z * NY + d) * 2 + c))
 
+    pairs = [
+        (ids_hbm, ids_ref), (gate_hbm, gate_ref), (x_hbm, x_ref), (klat_hbm, klat_ref), (krope_hbm, krope_ref),
+        (qrope_hbm, qrope_ref),
+    ]
+    small = [pltpu.make_async_copy(src, dst, sem_in.at[k]) for k, (src, dst) in enumerate(pairs)]
+    for copy in small:
+        copy.start()
     locals_ = [pltpu.make_async_copy(q_ref, ql.at[0], sem_l.at[0])]
     for k in range(NY):
         rows = pl.ds(k * COLS, COLS)
@@ -92,6 +100,8 @@
     for copy in locals_:
         copy.start()
 
+    for copy in small:
+        copy.wait()
     kbuf[0, 0, :, :LATENT] = klat_ref[...]
     kbuf[0, 0, :, LATENT:] = jnp.concatenate([krope_ref[...], jnp.zeros((KEYS, 128 - ROPE), bf16)], axis=1)
 
@@ -417,7 +427,6 @@
     qraw[0] = qrope_ref[...]
     ring(1)
     spread(0)
-    keep_rows()
     queries_on()
     ring(2)
     spread(2)
@@ -426,30 +435,31 @@
     share_rows(0)
     spread(3)
     share_rows(2)
+    ring(4)
+    keep_rows()
     weights_here()
-    ring(4)
     experts(0)
     share_rows(1)
     experts(2)
-    queries()
     ring(5)
     share_rows(3)
     combine(2)
     experts(1)
     combine(0)
-    attend(1, True)
     experts(3)
     ring(6)
-    attend(2, False)
     combine(3)
     combine(1)
     combine_far(0)
+    queries()
     give_back(2)
+    attend(1, True)
     ring(7)
+    attend(2, False)
+    combine_far(1)
     attend(3, False)
-    combine_far(1)
+    give_back(3)
     attend(4, False)
-    give_back(3)
     ring(8)
     attend(5, False)
     give_back(0)
@@ -481,7 +491,7 @@
             jax.ShapeDtypeStruct((ROWS, LATENT), bf16),
         ),
         in_specs=[
-            vmem, vmem, vmem, anywhere, anywhere, anywhere, anywhere, vmem, vmem, vmem,
+            anywhere, anywhere, anywhere, anywhere, anywhere, anywhere, anywhere, anywhere, anywhere, anywhere,
             pl.BlockSpec(memory_space=pltpu.SMEM),
         ],
         out_specs=(vmem, vmem),
@@ -534,6 +544,13 @@
             dma((2, QUART)), dma,
             dma((NY,)), dma,
             dma((NY, 3)), dma((1,)),
+            pltpu.VMEM((TOKENS, WIDTH), bf16),
+            pltpu.VMEM((2, TOKENS), jnp.int32),
+            pltpu.VMEM((2, TOKENS), f32),
+            pltpu.VMEM((TOKENS, HEADS * ROPE), bf16),
+            pltpu.VMEM((KEYS, LATENT), bf16),
+            pltpu.VMEM((KEYS, ROPE), bf16),
+            dma((6,)),
         ],
         compiler_params=pltpu.CompilerParams(
             collective_id=0, has_side_effects=True, vmem_limit_bytes=56 * 1024 * 1024

time: 78.1 us -> 77.1 us (0.987)
  Pallas kernels: 73.5 us -> 72.5 us
    pallas_call x1, Pallas kernels: 73.5 us -> 72.5 us  [per_device(): pl.pallas_call(kernel, out_shape=(jax.ShapeDtypeStruct((TOKENS, WIDTH), b...]
where the time goes in v4:
time: 77.1 us; the launch traced here: 76.9 us
  Pallas kernels  72.5 us (94%)
  local copies, waits for them, and re-layouts  3.11 us (4%)
  between operations  1.29 us (2%)
    pallas_call x1, Pallas kernels, per_device(): pl.pallas_call(kernel, out_shape=(jax.ShapeDtypeStruct((TOKENS, WIDTH), b...  72.5 us
    unnamed x2, local copies, waits for them, and re-layouts  3.11 us

profile of v4, /device:TPU:24, one launch (start us, length us, event | category | flops | bytes accessed | tf_op | source)
XLA Modules:
  0.0 76.9 jit_solution(2556494558351151019)
XLA Ops:
  1.3 72.5 %layer.1 = (bf16[8,3584]{1,0:T(8,128)(2,1)}, bf16[256,512]{1,0:T(8,128)(2,1)}) custom-call(bf16[8,3584]{1,0:T(8,128)(2,1)} %bitcast.23, s32[2,8]{1,0:T(2,128)} %bitcast.26, f32[2,8]{1,0:T(2,128)} %bitcast.27, bf16[3584,128]{1,0:T(8,128)(2,1)} %bitcast.18, bf16[3584,128]{1,0:T(8,128)(2,1)} %bitcast.19, bf16[128,3584]{1,0:T(8,128)(2,1)} %bitcast.20, ...), custom_call_target="tpu_custom_call" | custom-call | flops 6000000000 | bytes 4000000 | tf_op jit(solution)/shard_map/layer/pallas_call | solution.py:487
  73.8 1.4 %copy.16 = bf16[1,8,3584]{2,1,0:T(8,128)(2,1)} copy(bf16[1,8,3584]{2,1,0:T(8,128)(2,1)} %bitcast.17) | data formatting | bytes 114688
  75.2 1.7 %copy.17 = bf16[1,8,32,512]{3,2,1,0:T(8,128)(2,1)} copy(bf16[1,8,32,512]{3,2,1,0:T(8,128)(2,1)} %bitcast.16) | data formatting | bytes 524288
